TPU v7x, 128 devices: a whole 4x4x4 slice. The times are simulated.
128 devices in a mesh: group: 4 (over z), fsdp: 32 (over x, y, core).
Axes of the slice: x: 4, y: 4, z: 4, core: 2. Of those that a mesh axis runs over, the one named last changes fastest.
Arguments:
- gradient: bfloat16 [8192, 8192], P('fsdp', 'group'), may hold values from -135 to 135
- second_moment: float32 [8192, 8192], P('fsdp', 'group'), may hold values from 0.05 to 5
- left_root: float32 [4, 32, 2, 1024, 1024], P('group', 'fsdp'), may hold values from -3 to 3, as said below
- right_root: float32 [4, 32, 2, 1024, 1024], P('group', 'fsdp'), may hold values from -3 to 3, as said below
- block_rows: int32 [4, 16], replicated, may hold values from 0 to 7, as said below
- block_cols: int32 [4, 16], replicated, may hold values from 0 to 1, as said below
- block_owner: int32 [4, 16], replicated, may hold values from 0 to 31, as said below
Outputs:
- update: bfloat16 [8192, 8192], P('fsdp')
- moment: float32 [8192, 8192], P('fsdp', 'group')
Inputs may be any that keep to these rules, and one draw needn't show every extreme that they name: In each group, the pairs (block_rows, block_cols) over the list name every block of the 8 x 2 grid once. `block_cols`: see block_rows. `block_owner`: in each group a device owns at most 2 blocks, and exactly 2 for some device; a device owns at most one block of any block row and at most one of any block column. `left_root`: Symmetric. `right_root`: Symmetric.
All inputs are finite; a program needn't handle non-finite values.
Results may differ from a plain program's by a relative error of at most 0.001.
Values may be sent and summed in bfloat16 or wider, within the bound.
No kernel may reach another device: no remote copies, remote signals or barrier semaphores. Data moves between devices by JAX's collectives and lax.ppermute only.
A program may use at most 128 MiB of HBM per device.

v0:
```python
import jax
import jax.numpy as jnp
from jax import lax
from jax.sharding import PartitionSpec as P

BS = 1024


BETA_TWO = 0.999
ADAM_EPS = 1e-08
NORM_EPS = 1e-06


def on_device(gradient, second_moment, left_root, right_root, block_rows, block_cols, block_owner):
    shard_rows, width = gradient.shape
    col_blocks = width // BS
    fsdp_count = lax.axis_size("fsdp")
    fsdp_index = lax.axis_index("fsdp")
    group_index = lax.axis_index("group")
    contrib = BS // shard_rows
    row_count = fsdp_count // contrib
    slot_count = left_root.shape[2]
    list_len = block_rows.shape[1]
    grad_float = gradient.astype(jnp.float32)
    moment = BETA_TWO * second_moment + (1.0 - BETA_TWO) * grad_float * grad_float
    adam_dir = grad_float / (jnp.sqrt(moment) + ADAM_EPS)
    rows_list = lax.dynamic_index_in_dim(block_rows, group_index, 0, keepdims=False)
    cols_list = lax.dynamic_index_in_dim(block_cols, group_index, 0, keepdims=False)
    owner_list = lax.dynamic_index_in_dim(block_owner, group_index, 0, keepdims=False)
    home_row = fsdp_index // contrib
    col_range = jnp.arange(col_blocks, dtype=jnp.int32)
    row_range = jnp.arange(row_count, dtype=jnp.int32)
    targets = jnp.arange(fsdp_count, dtype=jnp.int32)
    in_home_row = rows_list == home_row
    col_match = cols_list[:, None] == col_range[None, :]
    partial_value = jnp.sum(jnp.square(adam_dir).reshape(shard_rows, col_blocks, BS), axis=(0, 2))
    local_table = jnp.sum(
        jnp.where(in_home_row[:, None] & col_match, partial_value[None, :], 0.0), axis=1
    )
    adam_sq = lax.psum(local_table, "fsdp")
    positions = jnp.arange(list_len, dtype=jnp.int32)
    same_owner = owner_list[None, :] == owner_list[:, None]
    slot_list = jnp.sum(
        (same_owner & (positions[None, :] < positions[:, None])).astype(jnp.int32), axis=1
    )
    slot_range = jnp.arange(slot_count, dtype=jnp.int32)
    owned = (owner_list[None, :] == fsdp_index) & (slot_list[None, :] == slot_range[:, None])
    slot_valid = jnp.any(owned, axis=1)
    slot_rows = jnp.sum(jnp.where(owned, rows_list[None, :], 0), axis=1)
    slot_norm = jnp.sum(jnp.where(owned, adam_sq[None, :], 0.0), axis=1)
    highest = lax.Precision.HIGHEST
    left_slots = left_root[0, 0]
    right_slots = right_root[0, 0]
    matches = (owner_list[None, :] == targets[:, None]) & in_home_row[None, :]
    choose_dest = jnp.dot(matches.astype(jnp.float32), col_match.astype(jnp.float32)).astype(
        jnp.bfloat16
    )
    outgoing = jnp.einsum(
        "dc,rcb->drb",
        choose_dest,
        gradient.reshape(shard_rows, col_blocks, BS),
        preferred_element_type=jnp.float32,
    ).astype(jnp.bfloat16)
    incoming = lax.all_to_all(outgoing, "fsdp", split_axis=0, concat_axis=0, tiled=True)
    row_blocks = incoming.reshape(row_count, BS, BS)
    slot_grads = jnp.take(row_blocks, slot_rows, axis=0).astype(jnp.float32)
    left_product = jnp.einsum("sij,sjk->sik", left_slots, slot_grads, precision=highest)
    precond = jnp.einsum("sij,sjk->sik", left_product, right_slots, precision=highest)
    shampoo_sq = jnp.sum(precond * precond, axis=(1, 2))
    ratio = jnp.sqrt(slot_norm / (shampoo_sq + NORM_EPS))
    updates = (ratio[:, None, None] * precond).astype(jnp.bfloat16)
    returns = (slot_valid[None, :] & (slot_rows[None, :] == row_range[:, None])).astype(
        jnp.bfloat16
    )
    replies = jnp.einsum(
        "rs,sjab->rjab",
        returns,
        updates.reshape(slot_count, contrib, shard_rows, BS),
        preferred_element_type=jnp.float32,
    ).astype(jnp.bfloat16)
    replies = replies.reshape(fsdp_count, shard_rows, BS)
    arrived = lax.all_to_all(replies, "fsdp", split_axis=0, concat_axis=0, tiled=True)
    own_update = jnp.einsum(
        "sc,sab->acb", choose_dest, arrived, preferred_element_type=jnp.float32
    ).astype(jnp.bfloat16)
    own_update = own_update.reshape(shard_rows, col_blocks * BS)
    update = lax.all_gather(own_update, "group", axis=1, tiled=True)
    return (update, moment)


def solution(mesh):
    placed = (
        P("fsdp", "group"),
        P("fsdp", "group"),
        P("group", "fsdp", None, None, None),
        P("group", "fsdp", None, None, None),
        P(),
        P(),
        P(),
    )
    return jax.shard_map(
        on_device,
        mesh=mesh,
        in_specs=placed,
        out_specs=(P("fsdp", None), P("fsdp", "group")),
        check_vma=False,
    )
```

profile of v0, /device:TPU:1, one launch (start us, length us, event | category | flops | bytes accessed | tf_op | source)
XLA Modules:
  0.0 681.9 jit_solution(16070529596623341069)
XLA Ops:
  7.2 0.7 copy-done
  7.9 0.7 fusion.34
  8.6 1.8 reshape.60
  10.4 0.7 compare_bitcast_fusion
  11.3 5.1 convolution_convert_fusion.1
  16.3 20.7 %copy.20 = bf16[32,256,1024]{2,1,0:T(8,128)(2,1)} copy(bf16[32,256,1024]{2,0,1:T(8,128)(2,1)S(1)} %convolution_convert_fusion.1) | data formatting | bytes 33554432 | tf_op jit(solution)/shard_map/convert_element_type | solution.py:63
  37.1 8.9 %all-to-all-start = ((bf16[32,256,1024]{2,1,0:T(8,128)(2,1)}), bf16[32,256,1024]{2,1,0:T(8,128)(2,1)}, u32[]{:S(2)}, u32[]{:S(2)}) async-start(bf16[32,256,1024]{2,1,0:T(8,128)(2,1)} %copy.20), calls=%async_computation | async-start | bytes 33554432 | tf_op jit(solution)/shard_map/all_to_all | solution.py:64
  46.1 2.5 fusion.13
  48.7 0.7 broadcast_compare_fusion
  49.4 253.8 %psum.7 = f32[16]{0:T(128)S(1)} all-reduce(f32[16]{0:T(128)S(1)} %fusion.26), channel_id=1, replica_groups=mesh['group'=4,'fsdp'=32] {'fsdp'}, use_global_device_ids=true, to_apply=%region_6.7 | all-reduce | flops 16 | bytes 128 | tf_op jit(solution)/shard_map/psum | solution.py:40
  303.3 0.2 convert_reduce_fusion
  303.9 11.6 %fusion.41 = (bf16[8,512,1024]{2,1,0:T(8,128)(2,1)}, bf16[8,512,1024]{2,1,0:T(8,128)(2,1)}) fusion(bf16[8,1024,1024]{2,1,0:T(8,128)(2,1)} %bitcast.8), kind=kLoop, calls=%fused_computation.65 | loop fusion | bytes 33554432 | tf_op jit(solution)/shard_map/jit(_take)/gather | solution.py:66
  315.5 4.1 gather_fusion
  319.6 5.4 gather_fusion.1
  324.9 18.3 %fusion.4 = f32[2,1024,1024]{1,2,0:T(8,128)} fusion(f32[1,1,2,1024,1024]{4,3,2,1,0:T(8,128)} %param.9, bf16[2,512,1024]{2,1,0:T(8,128)(2,1)} %gather_fusion.1, bf16[2,512,1024]{2,1,0:T(8,128)(2,1)S(1)} %gather_fusion, pred[2]{0:T(512)(128)(4,1)S(1)} %compare_and_fusion), kind=kOutput, calls=%fused_computation.8 | convolution fusion | flops 25780289536 | bytes 20971522 | tf_op jit(solution)/shard_map/sij,sjk->sik/dot_general | solution.py:67
  343.3 31.2 %multiply_reduce_fusion = (f32[2]{0:T(128)S(1)}, f32[2,1024,1024]{2,1,0:T(8,128)S(1)}) fusion(f32[2,1024,1024]{1,2,0:T(8,128)} %fusion.4, f32[1,1,2,1024,1024]{4,3,2,1,0:T(8,128)} %param.10), kind=kOutput, calls=%fused_computation.11 | convolution fusion | flops 25773998080 | bytes 25165832 | tf_op jit(solution)/shard_map/sij,sjk->sik/dot_general | solution.py:68
  374.5 1.3 multiply_convert_fusion
  375.9 6.4 convolution_convert_fusion
  382.3 20.7 %copy.24 = bf16[8,4,256,1024]{3,2,1,0:T(8,128)(2,1)} copy(bf16[8,4,256,1024]{3,0,2,1:T(8,128)(2,1)S(1)} %convolution_convert_fusion) | data formatting | bytes 33554432 | tf_op jit(solution)/shard_map/convert_element_type | solution.py:80
  403.0 203.2 %all_to_all.10 = bf16[32,256,1024]{2,1,0:T(8,128)(2,1)} all-to-all(bf16[32,256,1024]{2,1,0:T(8,128)(2,1)} %bitcast.40), channel_id=1, replica_groups=mesh['group'=4,'fsdp'=32] {'fsdp'}, dimensions={0} | all-to-all | bytes 33554432 | tf_op jit(solution)/shard_map/all_to_all | solution.py:82
  606.2 15.3 %fusion.14 = bf16[256,1024,2]{1,2,0:T(2,128)(2,1)S(1)} fusion(bf16[32,2,1]{0,1,2:T(2,128)(2,1)S(1)} %fusion.17, bf16[32,256,1024]{2,1,0:T(8,128)(2,1)} %all_to_all.10), kind=kOutput, calls=%fused_computation.23 | convolution fusion | flops 34078720 | bytes 17825920 | tf_op jit(solution)/shard_map/sc,sab->acb/dot_general | solution.py:83
  621.5 1.2 copy.29
  622.8 47.2 %all-gather.2.cloned.1.call-done = bf16[256,8192]{1,0:T(8,128)(2,1)} async-done(((bf16[256,2048]{1,0:T(8,128)(2,1)}), bf16[256,8192]{1,0:T(8,128)(2,1)}) %all-gather.2.cloned.1.call-update) | async-done | bytes 4194320 | tf_op jit(solution)/shard_map/all_gather | solution.py:87
  669.9 4.6 copy.37
  (30 shorter events, 0.8 us)
Async XLA Ops:
  7.2 0.7 copy-start
  7.9 3.3 copy-start.4
  8.5 2.6 copy-start.6
  37.1 9.0 %copy-start.2 = (bf16[256,2048]{1,0:T(8,128)(2,1)S(1)}, bf16[256,2048]{1,0:T(8,128)(2,1)}, u32[]{:S(2)}) copy-start(bf16[256,2048]{1,0:T(8,128)(2,1)} %param.7) | copy-start | bytes 3145732
  37.1 9.0 %copy-start.3 = (f32[256,2048]{1,0:T(8,128)S(1)}, f32[256,2048]{1,0:T(8,128)}, u32[]{:S(2)}) copy-start(f32[256,2048]{1,0:T(8,128)} %param.8) | copy-start | bytes 6291460
  37.1 12.3 %copy-start.5 = (s32[16]{0:T(128)S(1)}, s32[16]{0:T(128)}, u32[]{:S(2)}) copy-start(s32[16]{0:T(128)} %copy-done.4) | copy-start | bytes 196
  37.1 266.2 %copy-start.7 = (s32[16]{0:T(128)S(1)}, s32[16]{0:T(128)}, u32[]{:S(2)}) copy-start(s32[16]{0:T(128)} %copy-done.6) | copy-start | bytes 196
  37.1 266.8 %all-to-all-start = ((bf16[32,256,1024]{2,1,0:T(8,128)(2,1)}), bf16[32,256,1024]{2,1,0:T(8,128)(2,1)}, u32[]{:S(2)}, u32[]{:S(2)}) async-start(bf16[32,256,1024]{2,1,0:T(8,128)(2,1)} %copy.20), calls=%async_computation | async-start | bytes 33554432 | tf_op jit(solution)/shard_map/all_to_all | solution.py:64
  46.0 623.9 %all-gather.2.cloned.1.call-start = ((), (), s32[]{:S(2)}) async-start(), calls=%async_computation.2 | async-start | bytes 5242880 | tf_op jit(solution)/shard_map/all_gather | solution.py:87
  606.2 68.4 %copy-start.1 = (s32[4,16]{1,0:T(4,128)S(1)}, s32[4,16]{1,0:T(4,128)}, u32[]{:S(2)}) copy-start(s32[4,16]{1,0:T(4,128)} %param.12) | copy-start | bytes 772
Sparse Core Ops, SparseCore 0:
  622.9 47.0 all-gather.1
where the time goes:
time: 687 us; the launch traced here: 682 us
  blocking collectives  457 us (67%)
  matrix products  76.5 us (11%)
  local copies, waits for them, and re-layouts  71.5 us (10%)
  waiting for transfers between devices  47.2 us (7%)
  between operations  14.6 us (2%)
  starting transfers between devices  8.96 us (1%)
    psum x1, blocking collectives, on_device(): adam_sq = lax.psum(local_table, 'fsdp')  254 us
    all_to_all x1, blocking collectives, on_device(): lax.all_to_all(replies, 'fsdp', split_axis=0, concat_axis=0, tiled=True)  203 us
    all_gather x1, waiting for transfers between devices, on_device(): update = lax.all_gather(own_update, 'group', axis=1, tiled=True)  47.2 us
    dot_general x1, matrix products, on_device(): jnp.einsum('sij,sjk->sik', left_product, right_slots, precision=highest)  31.2 us
    gather x3, local copies, waits for them, and re-layouts, on_device(): slot_grads = jnp.take(row_blocks, slot_rows, axis=0).astype(jnp.float32)  21.1 us
    convert_element_type x1, local copies, waits for them, and re-layouts, on_device(): outgoing = jnp.einsum('dc,rcb->drb', choose_dest, gradient.reshape(shard_...  20.7 us
    convert_element_type x1, local copies, waits for them, and re-layouts, on_device(): replies = jnp.einsum('rs,sjab->rjab', returns, updates.reshape(slot_count...  20.7 us
    dot_general x1, matrix products, on_device(): jnp.einsum('sij,sjk->sik', left_slots, slot_grads, precision=highest)  18.3 us
  transfers between devices with their start and end apart: 2, of which 1 were waited for; matrix products, arithmetic and copies ran while one was open for 1% of the time, Pallas kernels for 0%

commit v1 on v0

v1 whole, which is shorter than its diff:
```python
import functools

import jax
import jax.numpy as jnp
from jax import lax
from jax.experimental import pallas as pl
from jax.experimental.pallas import tpu as pltpu
from jax.sharding import PartitionSpec as P

BS = 1024
BETA_TWO = 0.999
ADAM_EPS = 1e-08
NORM_EPS = 1e-06

ANY = pl.BlockSpec(memory_space=pl.ANY)
SMEM = pl.BlockSpec(memory_space=pltpu.SMEM)
MIB = 1 << 20


def run_copies(copies):
    for c in copies:
        c.start()
    for c in copies:
        c.wait()


def adam_kernel(g_ref, m_ref, mo_ref, part_ref):
    @pl.when(pl.program_id(0) == 0)
    def _():
        part_ref[...] = jnp.zeros_like(part_ref)

    g = g_ref[...].astype(jnp.float32)
    moment = BETA_TWO * m_ref[...] + (1.0 - BETA_TWO) * g * g
    mo_ref[...] = moment
    adam = g / (jnp.sqrt(moment) + ADAM_EPS)
    sq = adam * adam
    for b in range(sq.shape[1] // BS):
        s = jnp.sum(sq[:, b * BS : (b + 1) * BS].reshape(-1, 8, BS), axis=0)
        part_ref[:, b * BS : (b + 1) * BS] += s


def adam(gradient, second_moment):
    rows, width = gradient.shape
    tile = 64
    moment, part = pl.pallas_call(
        adam_kernel,
        grid=(rows // tile,),
        in_specs=[pl.BlockSpec((tile, width), lambda i: (i, 0))] * 2,
        out_specs=[pl.BlockSpec((tile, width), lambda i: (i, 0)), pl.BlockSpec((8, width), lambda i: (0, 0))],
        out_shape=[
            jax.ShapeDtypeStruct((rows, width), jnp.float32),
            jax.ShapeDtypeStruct((8, width), jnp.float32),
        ],
        compiler_params=pltpu.CompilerParams(vmem_limit_bytes=32 * MIB),
        name="adam",
    )(gradient, second_moment)
    return moment, jnp.sum(part.reshape(8, width // BS, BS), axis=(0, 2))


def split_kernel(slot_ref, l_ref, r_ref, lh_ref, ll_ref, rh_ref, rl_ref):
    for src, hi_ref, lo_ref in ((l_ref, lh_ref, ll_ref), (r_ref, rh_ref, rl_ref)):
        x = src[...]
        hi = x.astype(jnp.bfloat16)
        hi_ref[...] = hi
        lo_ref[...] = (x - hi.astype(jnp.float32)).astype(jnp.bfloat16)


def split_roots(slots, left, right):
    tile = 256
    spec_in = pl.BlockSpec((1, tile, BS), lambda b, i, s: (s[b], i, 0))
    spec_out = pl.BlockSpec((1, tile, BS), lambda b, i, s: (b, i, 0))
    return pl.pallas_call(
        split_kernel,
        grid_spec=pltpu.PrefetchScalarGridSpec(
            num_scalar_prefetch=1,
            grid=(2, BS // tile),
            in_specs=[spec_in] * 2,
            out_specs=[spec_out] * 4,
        ),
        out_shape=[jax.ShapeDtypeStruct((2, BS, BS), jnp.bfloat16)] * 4,
        compiler_params=pltpu.CompilerParams(vmem_limit_bytes=32 * MIB),
        name="split_roots",
    )(slots, left, right)


def pick_kernel(row_ref, src, dst, held, in_sem, sem):
    owners, cols = row_ref.shape
    run_copies([pltpu.make_async_copy(src, held, in_sem)])
    run_copies(
        [
            pltpu.make_async_copy(held.at[row_ref[d, b], :, b], dst.at[d, b], sem.at[d * cols + b])
            for d in range(owners)
            for b in range(cols)
        ]
    )


def pick_for_owners(row_of, spread):
    owners, cols = row_of.shape
    _, quarters, _, h, w = spread.shape
    return pl.pallas_call(
        pick_kernel,
        in_specs=[SMEM, ANY],
        out_specs=ANY,
        out_shape=jax.ShapeDtypeStruct((owners, cols, quarters, h, w), jnp.bfloat16),
        scratch_shapes=[
            pltpu.VMEM(spread.shape, jnp.bfloat16),
            pltpu.SemaphoreType.DMA,
            pltpu.SemaphoreType.DMA((owners * cols,)),
        ],
        name="pick_for_owners",
    )(row_of, spread)


def unpick_kernel(owner_ref, src, dst, held, sem, out_sem):
    rows, cols = owner_ref.shape
    run_copies(
        [
            pltpu.make_async_copy(src.at[owner_ref[r, b], b], held.at[r, :, b], sem.at[r * cols + b])
            for r in range(rows)
            for b in range(cols)
        ]
    )
    run_copies([pltpu.make_async_copy(held, dst, out_sem)])


def pick_from_owners(owner_of, got):
    rows, cols = owner_of.shape
    _, _, quarters, h, w = got.shape
    shape = (rows, quarters, cols, h, w)
    return pl.pallas_call(
        unpick_kernel,
        in_specs=[SMEM, ANY],
        out_specs=ANY,
        out_shape=jax.ShapeDtypeStruct(shape, jnp.bfloat16),
        scratch_shapes=[
            pltpu.VMEM(shape, jnp.bfloat16),
            pltpu.SemaphoreType.DMA((rows * cols,)),
            pltpu.SemaphoreType.DMA,
        ],
        name="pick_from_owners",
    )(owner_of, got)


def shampoo_kernel(valid_ref, norm_ref, lh, ll, rh, rl, g_in, out, g, lhv, llv, rhv, rlv, q, u, sem, osem):
    cols = g_in.shape[1]
    quarters = g_in.shape[2]
    h, w = g_in.shape[3:]
    parts = BS // w
    tile = 256

    for b in range(cols):

        @pl.when(valid_ref[b] > 0)
        def _(b=b):
            ins = []
            for k in range(quarters):
                for p in range(parts):
                    ins.append((g_in.at[pl.ds(p * (BS // quarters // h), BS // quarters // h), b, k], g.at[k, :, :, pl.ds(p * w, w)]))
            copies = [pltpu.make_async_copy(s, d, sem.at[n]) for n, (s, d) in enumerate(ins)]
            n = len(copies)
            copies += [
                pltpu.make_async_copy(s.at[b], d, sem.at[n + i])
                for i, (s, d) in enumerate(((lh, lhv), (ll, llv), (rh, rhv), (rl, rlv)))
            ]
            run_copies(copies)
            gv = g.reshape(BS, BS)

            def step(t, acc):
                rows = pl.ds(pl.multiple_of(t * tile, tile), tile)
                dot = functools.partial(jnp.dot, preferred_element_type=jnp.float32)
                p = dot(lhv[rows, :], gv[...]) + dot(llv[rows, :], gv[...])
                ph = p.astype(jnp.bfloat16)
                pl_ = (p - ph.astype(jnp.float32)).astype(jnp.bfloat16)
                qt = dot(ph, rhv[...]) + (dot(ph, rlv[...]) + dot(pl_, rhv[...]))
                q[rows, :] = qt
                return acc + jnp.sum((qt * qt).reshape(-1, 8, BS), axis=0)

            acc = lax.fori_loop(0, BS // tile, step, jnp.zeros((8, BS), jnp.float32))
            ratio = jnp.sqrt(norm_ref[b] / (jnp.sum(acc) + NORM_EPS))
            uv = u.reshape(BS, BS)

            def scale(t, c):
                rows = pl.ds(pl.multiple_of(t * 128, 128), 128)
                uv[rows, :] = (ratio * q[rows, :]).astype(jnp.bfloat16)
                return c

            lax.fori_loop(0, BS // 128, scale, 0)
            outs = []
            for k in range(quarters):
                for p in range(parts):
                    outs.append((u.at[k, :, :, pl.ds(p * w, w)], out.at[pl.ds(p * (BS // quarters // h), BS // quarters // h), b, k]))
            run_copies([pltpu.make_async_copy(s, d, osem.at[n]) for n, (s, d) in enumerate(outs)])


def shampoo(valid, norms, roots, got):
    big = (BS, BS)
    count = got.shape[2] * (BS // got.shape[4])
    four = (got.shape[2], BS // got.shape[2] // got.shape[3], got.shape[3], BS)
    return pl.pallas_call(
        shampoo_kernel,
        in_specs=[SMEM, SMEM] + [ANY] * 5,
        out_specs=ANY,
        out_shape=jax.ShapeDtypeStruct(got.shape, jnp.bfloat16),
        scratch_shapes=[pltpu.VMEM(four, jnp.bfloat16)]
        + [pltpu.VMEM(big, jnp.bfloat16)] * 4
        + [
            pltpu.VMEM(big, jnp.float32),
            pltpu.VMEM(four, jnp.bfloat16),
            pltpu.SemaphoreType.DMA((count + 4,)),
            pltpu.SemaphoreType.DMA((count,)),
        ],
        compiler_params=pltpu.CompilerParams(vmem_limit_bytes=48 * MIB),
        cost_estimate=pl.CostEstimate(flops=20 * BS**3, bytes_accessed=24 * MIB, transcendentals=0),
        name="shampoo",
    )(valid, norms, *roots, got)


def rows_kernel(place_ref, own, before, after, far_lo, far_hi, out, held, sem, out_sem):
    parts, cols, h, w = own.shape
    halves = BS // w
    depth = parts // halves
    copies = []
    n = 0
    for k, src in enumerate((own, before, after)):
        for b in range(cols):
            for p in range(halves):
                start = pl.multiple_of(place_ref[k] * (cols * BS) + (b * BS + p * w), w)
                copies.append(
                    pltpu.make_async_copy(src.at[pl.ds(p * depth, depth), b], held.at[:, :, pl.ds(start, w)], sem.at[n])
                )
                n += 1
    for p, src in enumerate((far_lo, far_hi)):
        for b in range(cols):
            start = pl.multiple_of(place_ref[3] * (cols * BS) + (b * BS + p * w), w)
            copies.append(pltpu.make_async_copy(src.at[:, b], held.at[:, :, pl.ds(start, w)], sem.at[n]))
            n += 1
    run_copies(copies)
    run_copies([pltpu.make_async_copy(held, out, out_sem)])


def gather_groups(pieces):
    parts, cols, h, w = pieces.shape
    halves = BS // w
    depth = parts // halves
    groups = lax.axis_size("group")
    me = lax.axis_index("group")
    up = [(i, (i + 1) % groups) for i in range(groups)]
    down = [(i, (i - 1) % groups) for i in range(groups)]
    before = lax.ppermute(pieces, "group", up)
    after = lax.ppermute(pieces, "group", down)
    far_lo = lax.ppermute(before[:depth], "group", up)
    far_hi = lax.ppermute(after[depth:], "group", down)
    place = jnp.stack([me, (me + groups - 1) % groups, (me + 1) % groups, (me + 2) % groups]).astype(jnp.int32)
    rows = pl.pallas_call(
        rows_kernel,
        in_specs=[SMEM] + [ANY] * 5,
        out_specs=ANY,
        out_shape=jax.ShapeDtypeStruct((depth, h, groups * cols * BS), jnp.bfloat16),
        scratch_shapes=[
            pltpu.VMEM((depth, h, groups * cols * BS), jnp.bfloat16),
            pltpu.SemaphoreType.DMA((4 * cols * halves,)),
            pltpu.SemaphoreType.DMA,
        ],
        compiler_params=pltpu.CompilerParams(vmem_limit_bytes=16 * MIB),
        name="whole_rows",
    )(place, pieces, before, after, far_lo, far_hi)
    return rows.reshape(depth * h, groups * cols * BS)


def gather_partials(partial):
    cols = partial.shape[0]
    wide = jnp.broadcast_to(jnp.pad(partial, (0, 128 - cols))[None, :], (8, 128))
    return lax.all_gather(wide, "fsdp", axis=0)[:, 0, :cols]


def on_device(gradient, second_moment, left_root, right_root, block_rows, block_cols, block_owner):
    shard_rows, width = gradient.shape
    cols = width // BS
    fsdp = lax.axis_size("fsdp")
    me = lax.axis_index("fsdp")
    group = lax.axis_index("group")
    quarters = BS // shard_rows
    row_count = fsdp // quarters
    h = 16
    halves = fsdp * h // shard_rows
    w = BS // halves
    pick = lambda t: lax.dynamic_index_in_dim(t, group, 0, keepdims=False)
    rows_list, cols_list, owner_list = pick(block_rows), pick(block_cols), pick(block_owner)

    count = rows_list.shape[0]
    pos = jnp.arange(count, dtype=jnp.int32)
    slot_list = jnp.sum((owner_list[None, :] == owner_list[:, None]) & (pos[None, :] < pos[:, None]), axis=1, dtype=jnp.int32)
    col_is = cols_list[None, :] == jnp.arange(cols, dtype=jnp.int32)[:, None]
    at_owner = (owner_list[None, None, :] == jnp.arange(fsdp, dtype=jnp.int32)[:, None, None]) & col_is[None]
    row_of = jnp.sum(jnp.where(at_owner, rows_list, 0), axis=2, dtype=jnp.int32)
    at_row = (rows_list[None, None, :] == jnp.arange(row_count, dtype=jnp.int32)[:, None, None]) & col_is[None]
    owner_of = jnp.sum(jnp.where(at_row, owner_list, 0), axis=2, dtype=jnp.int32)
    mine = (owner_list[None, :] == me) & col_is
    my_slot = jnp.sum(jnp.where(mine, slot_list, 0), axis=1, dtype=jnp.int32)
    my_row = jnp.sum(jnp.where(mine, rows_list, 0), axis=1, dtype=jnp.int32)
    my_valid = jnp.sum(mine, axis=1, dtype=jnp.int32)

    mixed = gradient.reshape(shard_rows // h, h, cols, halves, w).transpose(3, 0, 2, 1, 4)
    spread = lax.all_to_all(mixed.reshape(fsdp, cols, h, w), "fsdp", 0, 0, tiled=True)
    moment, partial = adam(gradient, second_moment)
    row_norm = jnp.sum(gather_partials(partial).reshape(row_count, quarters, cols), axis=1)
    norms = jnp.sum(
        jnp.where(my_row[None, :] == jnp.arange(row_count, dtype=jnp.int32)[:, None], row_norm, 0.0), axis=0
    )
    roots = split_roots(my_slot, left_root[0, 0], right_root[0, 0])

    send = pick_for_owners(row_of, spread.reshape(row_count, quarters, cols, h, w))
    got = lax.all_to_all(send, "fsdp", 0, 0, tiled=True)
    reply = shampoo(my_valid, norms, roots, got)
    back = lax.all_to_all(reply, "fsdp", 0, 0, tiled=True)
    home = pick_from_owners(owner_of, back)
    pieces = lax.all_to_all(home.reshape(fsdp, cols, h, w), "fsdp", 0, 0, tiled=True)
    return gather_groups(pieces), moment


def solution(mesh):
    placed = (
        P("fsdp", "group"),
        P("fsdp", "group"),
        P("group", "fsdp", None, None, None),
        P("group", "fsdp", None, None, None),
        P(),
        P(),
        P(),
    )
    return jax.shard_map(
        on_device,
        mesh=mesh,
        in_specs=placed,
        out_specs=(P("fsdp", None), P("fsdp", "group")),
        check_vma=False,
    )
```

time: 687 us -> 292 us (0.43)
  blocking collectives: 457 us -> 87 us
  matrix products: 76.5 us -> 0 us
  waiting for transfers between devices: 47.2 us -> 103 us
  local copies, waits for them, and re-layouts: 71.5 us -> 17.9 us
  starting transfers between devices: 8.96 us -> 58.4 us
  Pallas kernels: 0 us -> 23.8 us
  between operations: 14.6 us -> 0.81 us
    psum x1 -> x0, blocking collectives: 254 us -> none  [on_device(): adam_sq = lax.psum(local_table, 'fsdp')]
    all_to_all x1, blocking collectives: 203 us -> 24 us  [on_device(): lax.all_to_all(home.reshape(fsdp, cols, h, w), 'fsdp', 0, 0, tiled=True)]
    dot_general x6 -> x0, matrix products: 76.5 us -> none  [the longest x1 31.2 us: on_device(): jnp.einsum('sij,sjk->sik', left_product, right_slots, precision=highest)]
    all_to_all x1 -> x3, waiting for transfers between devices: 0.01 us -> 66.7 us  [the longest x1 51.4 us: on_device(): back = lax.all_to_all(reply, 'fsdp', 0, 0, tiled=True)]
    all_gather x0 -> x1, blocking collectives: none -> 62.9 us  [gather_partials(): return lax.all_gather(wide, 'fsdp', axis=0)[:, 0, :cols]]
    all_gather x1 -> x0, waiting for transfers between devices: 47.2 us -> none  [on_device(): update = lax.all_gather(own_update, 'group', axis=1, tiled=True)]
    all_to_all x1 -> x3, starting transfers between devices: 8.92 us -> 52.7 us  [the longest x1 39.2 us: on_device(): back = lax.all_to_all(reply, 'fsdp', 0, 0, tiled=True)]
    convert_element_type x2 -> x0, local copies, waits for them, and re-layouts: 41.4 us -> none  [the longest x1 20.7 us: on_device(): outgoing = jnp.einsum('dc,rcb->drb', choose_dest, gradient.reshape(shard_...]
  transfers between devices with their start and end apart: 2 -> 7, of which waited for: 1 -> 5; matrix products, arithmetic and copies ran while one was open for 1% -> 2% of each run, Pallas kernels for 0% -> 4%
where the time goes in v1:
time: 292 us
  waiting for transfers between devices  103 us (35%)
  blocking collectives  87 us (30%)
  starting transfers between devices  58.4 us (20%)
  Pallas kernels  23.8 us (8%)
  local copies, waits for them, and re-layouts  17.9 us (6%)
    all_gather x1, blocking collectives, gather_partials(): return lax.all_gather(wide, 'fsdp', axis=0)[:, 0, :cols]  62.9 us
    all_to_all x1, waiting for transfers between devices, on_device(): back = lax.all_to_all(reply, 'fsdp', 0, 0, tiled=True)  51.4 us
    all_to_all x1, starting transfers between devices, on_device(): back = lax.all_to_all(reply, 'fsdp', 0, 0, tiled=True)  39.2 us
    all_to_all x1, blocking collectives, on_device(): lax.all_to_all(home.reshape(fsdp, cols, h, w), 'fsdp', 0, 0, tiled=True)  24 us
    ppermute x1, waiting for transfers between devices, gather_groups(): after = lax.ppermute(pieces, 'group', down)  22.4 us
    all_to_all x1, waiting for transfers between devices, on_device(): lax.all_to_all(mixed.reshape(fsdp, cols, h, w), 'fsdp', 0, 0, tiled=True)  15.3 us
    unnamed x20, local copies, waits for them, and re-layouts  11 us
    ppermute x1, waiting for transfers between devices, gather_groups(): far_hi = lax.ppermute(after[depth:], 'group', down)  9.67 us
  transfers between devices with their start and end apart: 7, of which 5 were waited for; matrix products, arithmetic and copies ran while one was open for 2% of the time, Pallas kernels for 4%

profile of v1, /device:TPU:1, one launch (start us, length us, event | category | flops | bytes accessed | tf_op | source)
XLA Modules:
  0.0 291.6 jit_solution(12018448999433539478)
XLA Ops:
  0.6 1.8 reshape.94
  2.5 1.2 copy.16
  3.7 8.6 %all-to-all-start = ((bf16[32,2,16,512]{3,2,1,0:T(8,128)(2,1)}), bf16[32,2,16,512]{3,2,1,0:T(8,128)(2,1)S(1)}, u32[]{:S(2)}, u32[]{:S(2)}) async-start(bf16[32,2,16,512]{3,2,1,0:T(8,128)(2,1)} %bitcast.14), calls=%async_computation | async-start | bytes 2097152 | tf_op jit(solution)/shard_map/all_to_all | solution.py:305
  13.9 15.3 %all-to-all-done = bf16[32,2,16,512]{3,2,1,0:T(8,128)(2,1)S(1)} async-done(((bf16[32,2,16,512]{3,2,1,0:T(8,128)(2,1)}), bf16[32,2,16,512]{3,2,1,0:T(8,128)(2,1)S(1)}, u32[]{:S(2)}, u32[]{:S(2)}) %all-to-all-start) | async-done | bytes 1048608 | tf_op jit(solution)/shard_map/all_to_all | solution.py:305
  30.2 4.7 %pick_for_owners.1 = bf16[32,2,4,16,512]{4,3,2,1,0:T(8,128)(2,1)} custom-call(s32[32,2]{1,0:T(8,128)} %copy.17.row_ref, bf16[8,4,2,16,512]{4,3,2,1,0:T(8,128)(2,1)} %bitcast.26), custom_call_target="tpu_custom_call" | custom-call | tf_op jit(solution)/shard_map/pick_for_owners/pallas_call | solution.py:101
  34.9 4.9 %all-to-all-start.1 = ((bf16[32,2,4,16,512]{4,3,2,1,0:T(8,128)(2,1)}), bf16[32,2,4,16,512]{4,3,2,1,0:T(8,128)(2,1)}, u32[]{:S(2)}, u32[]{:S(2)}) async-start(bf16[32,2,4,16,512]{4,3,2,1,0:T(8,128)(2,1)} %pick_for_owners.1), calls=%async_computation.1 | async-start | bytes 8388608 | tf_op jit(solution)/shard_map/all_to_all | solution.py:314
  39.8 2.1 adam.1
  42.1 62.9 %all-gather.1 = f32[32,1,128]{2,1,0:T(1,128)S(1)} all-gather(f32[1,1,128]{2,1,0:T(1,128)S(1)} %pad_bitcast_fusion), channel_id=3, replica_groups=mesh['group'=4,'fsdp'=32] {'fsdp'}, dimensions={0}, use_global_device_ids=true | all-gather | bytes 16896 | tf_op jit(solution)/shard_map/all_gather | solution.py:274
  105.5 9.0 %split_roots.1 = (bf16[2,1024,1024]{2,1,0:T(8,128)(2,1)S(1)}, bf16[2,1024,1024]{2,1,0:T(8,128)(2,1)S(1)}, bf16[2,1024,1024]{2,1,0:T(8,128)(2,1)S(1)}, bf16[2,1024,1024]{2,1,0:T(8,128)(2,1)S(1)}) custom-call(s32[2]{0:T(128)S(1)} %get-tuple-element.14.slot_ref, f32[2,1024,1024]{2,1,0:T(8,128)} %bitcast.24, f32[2,1024,1024]{2,1,0:T(8,128)} %bitcast.25), custom_call_target="tpu_custom_call" | custom-call | tf_op jit(solution)/shard_map/split_roots/pallas_call | solution.py:72
  114.6 2.0 copy-done.3
  116.6 2.0 copy-done.4
  118.5 2.0 copy-done.5
  120.5 2.0 copy-done.6
  123.4 2.0 copy-done.1
  125.4 39.2 %all-to-all-start.2 = ((bf16[32,2,4,16,512]{4,3,2,1,0:T(8,128)(2,1)}), bf16[32,2,4,16,512]{4,3,2,1,0:T(8,128)(2,1)}, u32[]{:S(2)}, u32[]{:S(2)}) async-start(bf16[32,2,4,16,512]{4,3,2,1,0:T(8,128)(2,1)} %copy-done.1), calls=%async_computation.2 | async-start | bytes 8388608 | tf_op jit(solution)/shard_map/all_to_all | solution.py:316
  165.4 51.4 %all-to-all-done.2.src = bf16[32,2,4,16,512]{4,3,2,1,0:T(8,128)(2,1)} async-done(((bf16[32,2,4,16,512]{4,3,2,1,0:T(8,128)(2,1)}), bf16[32,2,4,16,512]{4,3,2,1,0:T(8,128)(2,1)}, u32[]{:S(2)}, u32[]{:S(2)}) %all-to-all-start.2) | async-done | bytes 4194336 | tf_op jit(solution)/shard_map/all_to_all | solution.py:316
  216.8 3.1 %pick_from_owners.1 = bf16[8,4,2,16,512]{4,3,2,1,0:T(8,128)(2,1)} custom-call(s32[8,2]{1,0:T(8,128)} %copy.18.owner_ref, bf16[32,2,4,16,512]{4,3,2,1,0:T(8,128)(2,1)} %all-to-all-done.2.src), custom_call_target="tpu_custom_call" | custom-call | tf_op jit(solution)/shard_map/pick_from_owners/pallas_call | solution.py:131
  219.9 24.0 %all_to_all.20.own = bf16[32,2,16,512]{3,2,1,0:T(8,128)(2,1)S(1)} all-to-all(bf16[32,2,16,512]{3,2,1,0:T(8,128)(2,1)} %bitcast.29), channel_id=1, replica_groups=mesh['group'=4,'fsdp'=32] {'fsdp'}, dimensions={0} | all-to-all | bytes 2097152 | tf_op jit(solution)/shard_map/all_to_all | solution.py:318
  243.9 2.3 collective-permute-start.1
  246.2 22.4 %collective-permute-done.1.after = bf16[32,2,16,512]{3,2,1,0:T(8,128)(2,1)S(1)} collective-permute-done((bf16[32,2,16,512]{3,2,1,0:T(8,128)(2,1)S(1)}, bf16[32,2,16,512]{3,2,1,0:T(8,128)(2,1)S(1)}, u32[]{:S(2)}, u32[]{:S(2)}) %collective-permute-start.1) | collective-permute-done | bytes 1048608 | tf_op jit(solution)/shard_map/ppermute | solution.py:251
  269.5 3.4 %collective-permute-start.3 = (bf16[16,2,16,512]{3,2,1,0:T(8,128)(2,1)}, bf16[16,2,16,512]{3,2,1,0:T(8,128)(2,1)}, u32[]{:S(2)}, u32[]{:S(2)}) collective-permute-start(bf16[16,2,16,512]{3,2,1,0:T(8,128)(2,1)} %slice.15), channel_id=1, source_target_pairs={{0,96},{32,0},{64,32},{96,64},{1,97},{33,1},{65,33},{97,65},{2,98}... | collective-permute-start | bytes 1572872 | tf_op jit(solution)/shard_map/ppermute | solution.py:253
  273.8 9.7 %collective-permute-done.3.far_hi = bf16[16,2,16,512]{3,2,1,0:T(8,128)(2,1)} collective-permute-done((bf16[16,2,16,512]{3,2,1,0:T(8,128)(2,1)}, bf16[16,2,16,512]{3,2,1,0:T(8,128)(2,1)}, u32[]{:S(2)}, u32[]{:S(2)}) %collective-permute-start.3) | collective-permute-done | bytes 524320 | tf_op jit(solution)/shard_map/ppermute | solution.py:253
  283.5 4.0 %collective-permute-done.2.far_lo = bf16[16,2,16,512]{3,2,1,0:T(8,128)(2,1)} collective-permute-done((bf16[16,2,16,512]{3,2,1,0:T(8,128)(2,1)}, bf16[16,2,16,512]{3,2,1,0:T(8,128)(2,1)}, u32[]{:S(2)}, u32[]{:S(2)}) %collective-permute-start.2) | collective-permute-done | bytes 524320 | tf_op jit(solution)/shard_map/ppermute | solution.py:252
  287.5 4.1 %whole_rows.1 = bf16[16,16,8192]{2,1,0:T(8,128)(2,1)} custom-call(s32[4]{0:T(128)S(1)} %pad_add_fusion.place_ref, bf16[32,2,16,512]{3,2,1,0:T(8,128)(2,1)S(1)} %all_to_all.20.own, bf16[32,2,16,512]{3,2,1,0:T(8,128)(2,1)S(1)} %collective-permute-done.before, bf16[32,2,16,512]{3,2,1,0:T(8,128)(2,1)S(1)} %collective-permute-done.1.after, ...), custom_call_target="tpu_custom_call" | custom-call | tf_op jit(solution)/shard_map/whole_rows/pallas_call | solution.py:255
  (40 shorter events, 6.7 us)
Async XLA Ops:
  0.6 11.7 %copy-start.8 = (s32[4,16]{1,0:T(4,128)S(1)}, s32[4,16]{1,0:T(4,128)}, u32[]{:S(2)}) copy-start(s32[4,16]{1,0:T(4,128)} %param.13) | copy-start | bytes 772
  3.7 25.5 %all-to-all-start = ((bf16[32,2,16,512]{3,2,1,0:T(8,128)(2,1)}), bf16[32,2,16,512]{3,2,1,0:T(8,128)(2,1)S(1)}, u32[]{:S(2)}, u32[]{:S(2)}) async-start(bf16[32,2,16,512]{3,2,1,0:T(8,128)(2,1)} %bitcast.14), calls=%async_computation | async-start | bytes 2097152 | tf_op jit(solution)/shard_map/all_to_all | solution.py:305
  29.2 1.0 copy-start.7
  34.9 5.0 %copy-start = (bf16[256,2048]{1,0:T(8,128)(2,1)S(1)}, bf16[256,2048]{1,0:T(8,128)(2,1)}, u32[]{:S(2)}) copy-start(bf16[256,2048]{1,0:T(8,128)(2,1)} %g_ref.1) | copy-start | bytes 3145732
  34.9 5.0 %copy-start.2 = (f32[256,2048]{1,0:T(8,128)S(1)}, f32[256,2048]{1,0:T(8,128)}, u32[]{:S(2)}) copy-start(f32[256,2048]{1,0:T(8,128)} %m_ref.1) | copy-start | bytes 6291460
  34.9 87.8 %all-to-all-start.1 = ((bf16[32,2,4,16,512]{4,3,2,1,0:T(8,128)(2,1)}), bf16[32,2,4,16,512]{4,3,2,1,0:T(8,128)(2,1)}, u32[]{:S(2)}, u32[]{:S(2)}) async-start(bf16[32,2,4,16,512]{4,3,2,1,0:T(8,128)(2,1)} %pick_for_owners.1), calls=%async_computation.1 | async-start | bytes 8388608 | tf_op jit(solution)/shard_map/all_to_all | solution.py:314
  114.5 2.0 copy-start.3
  116.6 2.0 copy-start.4
  118.5 2.0 copy-start.5
  120.5 2.0 copy-start.6
  123.4 2.0 copy-start.1
  125.4 91.4 %all-to-all-start.2 = ((bf16[32,2,4,16,512]{4,3,2,1,0:T(8,128)(2,1)}), bf16[32,2,4,16,512]{4,3,2,1,0:T(8,128)(2,1)}, u32[]{:S(2)}, u32[]{:S(2)}) async-start(bf16[32,2,4,16,512]{4,3,2,1,0:T(8,128)(2,1)} %copy-done.1), calls=%async_computation.2 | async-start | bytes 8388608 | tf_op jit(solution)/shard_map/all_to_all | solution.py:316
  243.9 24.7 %collective-permute-start.1 = (bf16[32,2,16,512]{3,2,1,0:T(8,128)(2,1)S(1)}, bf16[32,2,16,512]{3,2,1,0:T(8,128)(2,1)S(1)}, u32[]{:S(2)}, u32[]{:S(2)}) collective-permute-start(bf16[32,2,16,512]{3,2,1,0:T(8,128)(2,1)S(1)} %all_to_all.20.own), channel_id=1, source_target_pairs={{0,96},{32,0},{64,32},{96,64},{1,97},{33,1},{65,33},{97,65},{2,98}... | collective-permute-start | bytes 3145736 | tf_op jit(solution)/shard_map/ppermute | solution.py:251
  246.2 26.7 %collective-permute-start = (bf16[32,2,16,512]{3,2,1,0:T(8,128)(2,1)S(1)}, bf16[32,2,16,512]{3,2,1,0:T(8,128)(2,1)S(1)}, u32[]{:S(2)}, u32[]{:S(2)}) collective-permute-start(bf16[32,2,16,512]{3,2,1,0:T(8,128)(2,1)S(1)} %all_to_all.20.own), channel_id=1, source_target_pairs={{0,32},{32,64},{64,96},{96,0},{1,33},{33,65},{65,97},{97,1},{2,34}... | collective-permute-start | bytes 3145736 | tf_op jit(solution)/shard_map/ppermute | solution.py:250
  269.5 14.0 %collective-permute-start.3 = (bf16[16,2,16,512]{3,2,1,0:T(8,128)(2,1)}, bf16[16,2,16,512]{3,2,1,0:T(8,128)(2,1)}, u32[]{:S(2)}, u32[]{:S(2)}) collective-permute-start(bf16[16,2,16,512]{3,2,1,0:T(8,128)(2,1)} %slice.15), channel_id=1, source_target_pairs={{0,96},{32,0},{64,32},{96,64},{1,97},{33,1},{65,33},{97,65},{2,98}... | collective-permute-start | bytes 1572872 | tf_op jit(solution)/shard_map/ppermute | solution.py:253
  273.7 13.7 %collective-permute-start.2 = (bf16[16,2,16,512]{3,2,1,0:T(8,128)(2,1)}, bf16[16,2,16,512]{3,2,1,0:T(8,128)(2,1)}, u32[]{:S(2)}, u32[]{:S(2)}) collective-permute-start(bf16[16,2,16,512]{3,2,1,0:T(8,128)(2,1)} %slice.14), channel_id=1, source_target_pairs={{0,32},{32,64},{64,96},{96,0},{1,33},{33,65},{65,97},{97,1},{2,34}... | collective-permute-start | bytes 1572872 | tf_op jit(solution)/shard_map/ppermute | solution.py:252

commit v2 on v0

v2 whole, which is shorter than its diff:
```python
import functools

import jax
import jax.numpy as jnp
from jax import lax
from jax.experimental import pallas as pl
from jax.experimental.pallas import tpu as pltpu
from jax.sharding import PartitionSpec as P

BS = 1024
BETA_TWO = 0.999
ADAM_EPS = 1e-08
NORM_EPS = 1e-06

ANY = pl.BlockSpec(memory_space=pl.ANY)
SMEM = pl.BlockSpec(memory_space=pltpu.SMEM)
MIB = 1 << 20


def run_copies(copies):
    for c in copies:
        c.start()
    for c in copies:
        c.wait()


def adam_kernel(g_ref, m_ref, mo_ref, norm_ref, acc):
    step, cols = pl.program_id(0), acc.shape[1] // BS

    @pl.when(step == 0)
    def _():
        acc[...] = jnp.zeros_like(acc)

    g = g_ref[...].astype(jnp.float32)
    moment = BETA_TWO * m_ref[...] + (1.0 - BETA_TWO) * g * g
    mo_ref[...] = moment
    adam = g / (jnp.sqrt(moment) + ADAM_EPS)
    acc[...] += jnp.sum((adam * adam).reshape(-1, 8, acc.shape[1]), axis=0)

    @pl.when(step == pl.num_programs(0) - 1)
    def _():
        row = lax.broadcasted_iota(jnp.int32, norm_ref.shape, 0)
        lane = lax.broadcasted_iota(jnp.int32, norm_ref.shape, 1)
        rest = jnp.zeros(norm_ref.shape, jnp.float32)
        for b in range(cols):
            rest = jnp.where(lane == b, jnp.sum(acc[:, b * BS : (b + 1) * BS]), rest)
        out = jnp.zeros(norm_ref.shape, jnp.float32)
        for term in range(3):
            now = rest.astype(jnp.bfloat16).astype(jnp.float32)
            out = jnp.where(row == term, now, out)
            rest = rest - now
        norm_ref[...] = out.astype(jnp.bfloat16)


def adam(gradient, second_moment):
    rows, width = gradient.shape
    tile = 64
    return pl.pallas_call(
        adam_kernel,
        grid=(rows // tile,),
        in_specs=[pl.BlockSpec((tile, width), lambda i: (i, 0))] * 2,
        out_specs=[pl.BlockSpec((tile, width), lambda i: (i, 0)), pl.BlockSpec((16, 128), lambda i: (0, 0))],
        out_shape=[
            jax.ShapeDtypeStruct((rows, width), jnp.float32),
            jax.ShapeDtypeStruct((16, 128), jnp.bfloat16),
        ],
        scratch_shapes=[pltpu.VMEM((8, width), jnp.float32)],
        compiler_params=pltpu.CompilerParams(vmem_limit_bytes=56 * MIB),
        name="adam",
    )(gradient, second_moment)


RING = 4


def tables_kernel(rows_ref, cols_ref, owner_ref, place_ref, spread, fwd0, fwd1, back0, back1, from0, from1, offs, mine, far, row_of, owner_of):
    count = rows_ref.shape[1]
    devices, cols = row_of.shape
    me, group = place_ref[0], place_ref[1]
    for b in range(cols):
        for r in range(owner_of.shape[0]):
            owner_of[r, b] = 0
        for d in range(devices):
            row_of[d, b] = 0
        mine[0, b] = 0
        mine[1, b] = 0
        mine[2, b] = 0
    seen = jnp.int32(0)
    for k in range(count):
        r, b, o = rows_ref[group, k], cols_ref[group, k], owner_ref[group, k]
        row_of[o, b] = r
        owner_of[r, b] = o

        @pl.when(o == me)
        def _(r=r, b=b, seen=seen):
            mine[0, b] = seen
            mine[1, b] = 1
            mine[2, b] = r

        seen = seen + (o == me).astype(jnp.int32)

    c = me % 2
    y = (me // 2) % RING
    x = me // (2 * RING)
    yh, yl = y // 2, y % 2
    upper = c == 0
    sel = lambda a, b: jnp.where(upper, a, b)
    p_first, p_second = sel(x, y), sel(y, x)
    wrap = lambda v: (v + 2 * RING) % RING
    spread[0] = c
    sent = []
    for k, place in enumerate((2 * yh, 2 - 2 * yh, 2 * yh + 1, 3 - 2 * yh)):
        sent.append(sel(place, wrap(x + k)))
        spread[1 + k] = sent[k]
        spread[5 + k] = sel(place, wrap(x - k))
    for b, fwd in enumerate((fwd0, fwd1)):
        for flip in range(2):
            for k in range(RING):
                to = wrap(p_second + k)
                core = jnp.where(upper, flip, 1 - flip)
                row = row_of[sel((x * RING + to) * 2 + core, (to * RING + y) * 2 + core), b]
                for t in range(2):
                    n = (flip * RING + k) * 2 + t
                    inner = 2 * (row % 2) + t
                    fwd[0, n] = wrap(p_first - sel(row // 2, inner))
                    fwd[1, n] = sel(inner, row // 2)
    for b, (back, frm) in enumerate(((back0, from0), (back1, from1))):
        for k in range(RING):
            to = wrap(p_first + k)
            for u in range(4):
                owner = owner_of[sel(to * 2 + u // 2, u * 2 + to // 2), b]
                ox, oy, oc = owner // (2 * RING), (owner // 2) % RING, owner % 2
                back[0, k * 4 + u] = jnp.where(oc == c, 0, RING) + wrap(sel(oy, ox) - p_second)
                back[1, k * 4 + u] = sel(u % 2, to % 2)
        for k in range(4):
            owner = owner_of[sel(2 * x + sent[k] // 2, sent[k] * 2 + yh), b]
            ox, oy = owner // (2 * RING), (owner // 2) % RING
            frm[0, k] = wrap(p_first - sel(ox, oy))
            frm[1, k] = sent[k]
    for flip in range(2):
        from_upper = c == flip
        for k in range(RING):
            y_from, x_from = wrap(y - k), wrap(x - k)
            for t in range(2):
                for e in range(2):
                    up = ((y_from % 2) * 2 + e) * 256 + (y_from // 2) * 64 + t * 32
                    low = (t * 2 + e) * 256 + 128 + x_from * 32
                    offs[((flip * RING + k) * 2 + t) * 2 + e] = jnp.where(from_upper, up, low)
    for i, step in enumerate((0, 0, 3, 3, 1, 1, 2, 2)):
        far[0, i] = (group + step) % 4
        far[1, i] = c if i % 2 == 0 else 1 - c


def make_tables(rows, cols, owner, place, devices, col_count, row_count):
    i32 = lambda *shape: jax.ShapeDtypeStruct(shape, jnp.int32)
    shapes = [i32(9)] + [i32(2, 16)] * 4 + [i32(2, 4)] * 2 + [i32(32), i32(3, col_count), i32(2, 8)]
    shapes += [i32(devices, col_count), i32(row_count, col_count)]
    return pl.pallas_call(
        tables_kernel,
        in_specs=[SMEM] * 4,
        out_specs=[SMEM] * len(shapes),
        out_shape=shapes,
        name="tables",
    )(rows, cols, owner, place)


def stage_all(bufs, held, sems):
    copies = [pltpu.make_async_copy(src, held.at[i], sems.at[i]) for i, src in enumerate(bufs)]
    run_copies(copies)


def table_mover(name, table, ins, outs, pieces, piece_shape):
    n_in, n_out = len(ins), len(outs)

    def kernel(tab, *refs):
        srcs, dsts = refs[:n_in], refs[n_in : n_in + n_out]
        held, in_sem, out_sem = refs[n_in + n_out :]
        plan = pieces(tab, srcs, dsts)
        for i, (choices, _) in enumerate(plan):
            for cond, src in choices:
                copy = pltpu.make_async_copy(src, held.at[i], in_sem.at[i])
                if cond is None:
                    copy.start()
                else:
                    pl.when(cond)(copy.start)
        for i, (choices, dst) in enumerate(plan):
            pltpu.make_async_copy(choices[0][1], held.at[i], in_sem.at[i]).wait()
            pltpu.make_async_copy(held.at[i], dst, out_sem.at[i]).start()
        for i, (_, dst) in enumerate(plan):
            pltpu.make_async_copy(held.at[i], dst, out_sem.at[i]).wait()

    count = pieces.count
    size = 2 * count
    for d in piece_shape:
        size *= d
    return pl.pallas_call(
        kernel,
        in_specs=[SMEM] + [ANY] * n_in,
        out_specs=[ANY] * n_out,
        out_shape=[jax.ShapeDtypeStruct(o, jnp.bfloat16) for o in outs],
        scratch_shapes=[
            pltpu.VMEM((count, *piece_shape), jnp.bfloat16),
            pltpu.SemaphoreType.DMA((count,)),
            pltpu.SemaphoreType.DMA((count,)),
        ],
        compiler_params=pltpu.CompilerParams(vmem_limit_bytes=16 * MIB),
        cost_estimate=pl.CostEstimate(flops=0, bytes_accessed=2 * size, transcendentals=0),
        name=name,
    )(table, *ins)


def counted(count):
    def mark(f):
        f.count = count
        return f

    return mark


def picker(name, table, bufs, out_groups, outs_per, piece_shape, src_b=None, dst_b=None, before=()):
    n_in = len(bufs)
    per_buf = bufs[0].shape[0 if src_b is None else 1]

    def kernel(tab, *refs):
        srcs, dsts = refs[:n_in], refs[n_in + len(before) :][:out_groups]
        held, in_sem, out_sem = refs[n_in + len(before) + out_groups :]
        run_copies(
            [
                pltpu.make_async_copy(src if src_b is None else src.at[src_b], held.at[i], in_sem.at[i])
                for i, src in enumerate(srcs)
            ]
        )
        run_copies(
            [
                pltpu.make_async_copy(
                    held.at[tab[0, i * outs_per + j], tab[1, i * outs_per + j]],
                    dsts[i].at[j] if dst_b is None else dsts[i].at[dst_b, j],
                    out_sem.at[i * outs_per + j],
                )
                for i in range(out_groups)
                for j in range(outs_per)
            ]
        )

    size = 2
    for d in piece_shape:
        size *= d
    lead = () if dst_b is None else (2,)
    return pl.pallas_call(
        kernel,
        in_specs=[SMEM] + [ANY] * (n_in + len(before)),
        out_specs=[ANY] * out_groups,
        out_shape=[jax.ShapeDtypeStruct((*lead, outs_per, *piece_shape), jnp.bfloat16)] * out_groups,
        input_output_aliases={1 + n_in + i: i for i in range(len(before))},
        scratch_shapes=[
            pltpu.VMEM((n_in, per_buf, *piece_shape), jnp.bfloat16),
            pltpu.SemaphoreType.DMA((n_in,)),
            pltpu.SemaphoreType.DMA((out_groups * outs_per,)),
        ],
        compiler_params=pltpu.CompilerParams(vmem_limit_bytes=16 * MIB),
        cost_estimate=pl.CostEstimate(
            flops=0, bytes_accessed=size * (n_in * per_buf + out_groups * outs_per), transcendentals=0
        ),
        name=name,
    )(table, *bufs, *before)


def halves(v):
    hi = v.astype(jnp.bfloat16)
    return hi, (v - hi.astype(jnp.float32)).astype(jnp.bfloat16)


def column_copies(buf, box, to_box, sem):
    h, w = 64, 128
    depth, quarters = 4, 4
    made = []
    for k in range(quarters):
        for p in range(BS // w):
            away = buf.at[pl.ds(p * depth, depth), pl.ds(k * h, h), :]
            here = box.reshape(quarters, depth, h, BS).at[k, :, :, pl.ds(p * w, w)]
            n = k * (BS // w) + p
            made.append(pltpu.make_async_copy(*((away, here) if to_box else (here, away)), sem.at[n]))
    return made


def ring_copies(bufs, box, off_ref, to_box, sem):
    made = []
    for j, buf in enumerate(bufs):
        for t in range(2):
            for e in range(2):
                n = j * 4 + t * 2 + e
                here = box.at[pl.ds(pl.multiple_of(off_ref[n], 32), 32), :]
                away = buf.at[t, e]
                made.append(pltpu.make_async_copy(*((away, here) if to_box else (here, away)), sem.at[n]))
    return made


def shampoo_kernel(b, n_bufs, mine_ref, off_ref, norm_ref, left_ref, right_ref, *refs):
    ins, outs = refs[:n_bufs], refs[n_bufs : 2 * n_bufs]
    g, lv, rv, rhv, rlv, q, u, acc, norms, g_sem, root_sem, norm_sem, out_sem = refs[2 * n_bufs :]
    tile = 256
    tiles = BS // tile
    slot = mine_ref[0, b]

    def left_load(t):
        rows = pl.ds(pl.multiple_of(t * tile, tile), tile)
        return pltpu.make_async_copy(left_ref.at[0, 0, slot, rows, :], lv.at[rows, :], root_sem.at[t])

    right_load = pltpu.make_async_copy(right_ref.at[0, 0, slot], rv, root_sem.at[tiles])

    def moves(bufs, box, to_box, sem):
        if n_bufs == 1:
            return column_copies(bufs[0], box, to_box, sem)
        return ring_copies(bufs, box, off_ref, to_box, sem)

    norm_load = pltpu.make_async_copy(norm_ref.at[:, pl.ds(256, 16), :], norms, norm_sem)
    dot = functools.partial(jnp.dot, preferred_element_type=jnp.float32)

    @pl.when(mine_ref[1, b] > 0)
    def _():
        grads = moves(ins, g, True, g_sem)
        left_load(0).start()
        for c in grads:
            c.start()
        for t in range(1, tiles):
            left_load(t).start()
        right_load.start()
        norm_load.start()
        for c in grads:
            c.wait()
        acc[...] = jnp.zeros_like(acc)

        def step(t, carry):
            rows = pl.ds(pl.multiple_of(t * tile, tile), tile)
            left_load(t).wait()
            lh, ll = halves(lv[rows, :])
            ph, plow = halves(dot(lh, g[...]) + dot(ll, g[...]))

            @pl.when(t == 0)
            def _():
                right_load.wait()

                def split(i, carry):
                    part = pl.ds(pl.multiple_of(i * 128, 128), 128)
                    rhv[part, :], rlv[part, :] = halves(rv[part, :])
                    return carry

                lax.fori_loop(0, BS // 128, split, 0)

            qt = dot(ph, rhv[...]) + (dot(ph, rlv[...]) + dot(plow, rhv[...]))
            q[rows, :] = qt
            acc[...] += jnp.sum((qt * qt).reshape(-1, 8, BS), axis=0)
            return carry

        lax.fori_loop(0, tiles, step, 0)
        norm_load.wait()
        device = lax.broadcasted_iota(jnp.int32, norms.shape, 0)
        lane = lax.broadcasted_iota(jnp.int32, norms.shape, 2)
        wanted = (device // 4 == mine_ref[2, b]) & (lane == b)
        adam_sq = jnp.sum(jnp.where(wanted, norms[...].astype(jnp.float32), 0.0))
        ratio = jnp.sqrt(adam_sq / (jnp.sum(acc[...]) + NORM_EPS))

        def scale(t, carry):
            rows = pl.ds(pl.multiple_of(t * 128, 128), 128)
            u[rows, :] = (ratio * q[rows, :]).astype(jnp.bfloat16)
            return carry

        lax.fori_loop(0, BS // 128, scale, 0)
        run_copies(moves(outs, u, False, out_sem))


def shampoo(b, mine, offsets, norms, left_root, right_root, bufs, out):
    big = (BS, BS)
    return pl.pallas_call(
        functools.partial(shampoo_kernel, b, len(bufs)),
        in_specs=[SMEM] * 2 + [ANY] * (3 + len(bufs)),
        out_specs=[ANY] * len(bufs),
        out_shape=[jax.ShapeDtypeStruct(out, jnp.bfloat16)] * len(bufs),
        scratch_shapes=[
            pltpu.VMEM(big, jnp.bfloat16),
            pltpu.VMEM(big, jnp.float32),
            pltpu.VMEM(big, jnp.float32),
            pltpu.VMEM(big, jnp.bfloat16),
            pltpu.VMEM(big, jnp.bfloat16),
            pltpu.VMEM(big, jnp.float32),
            pltpu.VMEM(big, jnp.bfloat16),
            pltpu.VMEM((8, BS), jnp.float32),
            pltpu.VMEM((norms.shape[0], 16, 128), jnp.bfloat16),
            pltpu.SemaphoreType.DMA((32,)),
            pltpu.SemaphoreType.DMA((8,)),
            pltpu.SemaphoreType.DMA,
            pltpu.SemaphoreType.DMA((32,)),
        ],
        compiler_params=pltpu.CompilerParams(vmem_limit_bytes=58 * MIB),
        cost_estimate=pl.CostEstimate(flops=10 * BS**3, bytes_accessed=12 * MIB, transcendentals=0),
        name="shampoo",
    )(mine, offsets, norms, left_root, right_root, *bufs)


def pick_kernel(b, row_ref, src, norm, dst, held, sent, in_sem, norm_sem, sem):
    owners, (_, h, _) = row_ref.shape[0], src.shape
    run_copies([pltpu.make_async_copy(src, held, in_sem), pltpu.make_async_copy(norm, sent, norm_sem)])
    run_copies(
        [
            pltpu.make_async_copy(held.at[row_ref[d, b]], dst.at[d, pl.ds(0, h), :], sem.at[0, d])
            for d in range(owners)
        ]
        + [pltpu.make_async_copy(sent, dst.at[d, pl.ds(h, sent.shape[0]), :], sem.at[1, d]) for d in range(owners)]
    )


def pick_for_owners(b, row_of, spread, norm):
    owners = row_of.shape[0]
    _, h, w = spread.shape
    return pl.pallas_call(
        functools.partial(pick_kernel, b),
        in_specs=[SMEM, ANY, ANY],
        out_specs=ANY,
        out_shape=jax.ShapeDtypeStruct((owners, h + norm.shape[0], w), jnp.bfloat16),
        scratch_shapes=[
            pltpu.VMEM(spread.shape, jnp.bfloat16),
            pltpu.VMEM(norm.shape, jnp.bfloat16),
            pltpu.SemaphoreType.DMA,
            pltpu.SemaphoreType.DMA,
            pltpu.SemaphoreType.DMA((2, owners)),
        ],
        compiler_params=pltpu.CompilerParams(vmem_limit_bytes=16 * MIB),
        cost_estimate=pl.CostEstimate(flops=0, bytes_accessed=3 * MIB, transcendentals=0),
        name="pick_for_owners",
    )(row_of, spread, norm)


def unpick_kernel(b, owner_ref, src, dst, held, sem, out_sem):
    rows = owner_ref.shape[0]
    run_copies([pltpu.make_async_copy(src.at[owner_ref[r, b]], held.at[r], sem.at[r]) for r in range(rows)])
    run_copies([pltpu.make_async_copy(held, dst, out_sem)])


def pick_from_owners(b, owner_of, got):
    shape = (owner_of.shape[0], *got.shape[1:])
    return pl.pallas_call(
        functools.partial(unpick_kernel, b),
        in_specs=[SMEM, ANY],
        out_specs=ANY,
        out_shape=jax.ShapeDtypeStruct(shape, jnp.bfloat16),
        scratch_shapes=[
            pltpu.VMEM(shape, jnp.bfloat16),
            pltpu.SemaphoreType.DMA((shape[0],)),
            pltpu.SemaphoreType.DMA,
        ],
        compiler_params=pltpu.CompilerParams(vmem_limit_bytes=16 * MIB),
        cost_estimate=pl.CostEstimate(flops=0, bytes_accessed=1 * MIB, transcendentals=0),
        name="pick_from_owners",
    )(owner_of, got)


def column_rows_kernel(b, cols, tab, own, before, after, far_lo, far_hi, out, held, sem, out_sem):
    parts, h, w = own.shape
    sides = BS // w
    depth = parts // sides
    copies = []
    for k, src in enumerate((own, before, after)):
        for p in range(sides):
            copies.append((src.at[pl.ds(p * depth, depth)], held.at[k, :, :, pl.ds(p * w, w)]))
    for half, src in enumerate((far_lo, far_hi)):
        for p in range(sides // 2):
            lanes = pl.ds((half * (sides // 2) + p) * w, w)
            copies.append((src.at[pl.ds(p * depth, depth)], held.at[3, :, :, lanes]))
    run_copies([pltpu.make_async_copy(s, d, sem.at[n]) for n, (s, d) in enumerate(copies)])
    puts = []
    for k, i in enumerate((0, 2, 4, 6)):
        col = pl.multiple_of(tab[0, i] * (cols * BS) + b * BS, BS)
        puts.append(
            pltpu.make_async_copy(held.at[k].reshape(depth * h, BS), out.at[:, pl.ds(col, BS)], out_sem.at[k])
        )
    run_copies(puts)


def column_rows(b, cols, groups, table, bufs):
    parts, h, w = bufs[0].shape
    depth = parts * w // BS
    return pl.pallas_call(
        functools.partial(column_rows_kernel, b, cols),
        in_specs=[SMEM] + [ANY] * 5,
        out_specs=ANY,
        out_shape=jax.ShapeDtypeStruct((depth * h, groups * cols * BS), jnp.bfloat16),
        scratch_shapes=[
            pltpu.VMEM((4, depth, h, BS), jnp.bfloat16),
            pltpu.SemaphoreType.DMA((4 * BS // w,)),
            pltpu.SemaphoreType.DMA((4,)),
        ],
        compiler_params=pltpu.CompilerParams(vmem_limit_bytes=16 * MIB),
        cost_estimate=pl.CostEstimate(flops=0, bytes_accessed=4 * MIB, transcendentals=0),
        name="column_rows",
    )(table, *bufs)


def rows_kernel(b, cols, tab, *refs):
    ins, out = refs[:8], refs[-4]
    held, in_sem, out_sem = refs[-3:]
    h = ins[0].shape[0]
    copies = [pltpu.make_async_copy(src, held.at[i], in_sem.at[i]) for i, src in enumerate(ins)]
    for c in copies:
        c.start()
    puts = []
    for i in range(8):
        row = pl.multiple_of(tab[1, i] * h, h)
        col = pl.multiple_of(tab[0, i] * (cols * BS) + b * BS, BS)
        copies[i].wait()
        put = pltpu.make_async_copy(held.at[i], out.at[pl.ds(row, h), pl.ds(col, BS)], out_sem.at[i])
        put.start()
        puts.append(put)
    for put in puts:
        put.wait()


def whole_rows(b, cols, groups, table, bufs, before):
    h = bufs[0].shape[0]
    shape = jax.ShapeDtypeStruct((2 * h, groups * cols * BS), jnp.bfloat16)
    extra = [] if before is None else [before]
    return pl.pallas_call(
        functools.partial(rows_kernel, b, cols),
        in_specs=[SMEM] + [ANY] * (8 + len(extra)),
        out_specs=ANY,
        out_shape=shape,
        input_output_aliases={9: 0} if extra else {},
        scratch_shapes=[
            pltpu.VMEM((8, h, BS), jnp.bfloat16),
            pltpu.SemaphoreType.DMA((8,)),
            pltpu.SemaphoreType.DMA((8,)),
        ],
        compiler_params=pltpu.CompilerParams(vmem_limit_bytes=16 * MIB),
        cost_estimate=pl.CostEstimate(flops=0, bytes_accessed=4 * MIB, transcendentals=0),
        name="whole_rows",
    )(table, *bufs, *extra)


def permute(value, move):
    pairs = []
    for x in range(RING):
        for y in range(RING):
            for c in range(2):
                to = move(x, y, c)
                if to is not None:
                    tx, ty, tc = to
                    pairs.append(((x * RING + y) * 2 + c, ((tx % RING) * RING + ty % RING) * 2 + tc))
    return lax.ppermute(value, "fsdp", pairs)


def swap_cores(value):
    return permute(value, lambda x, y, c: (x, y, 1 - c))


def along_first(value, k):
    return permute(value, lambda x, y, c: (x + k, y, c) if c == 0 else (x, y + k, c))


def along_second(value, k, flip):
    return permute(value, lambda x, y, c: (x, y + k, c ^ flip) if c == 0 else (x + k, y, c ^ flip))


def back_second(value, k, flip):
    return permute(value, lambda x, y, c: (x, y - k, c ^ flip) if c ^ flip == 0 else (x - k, y, c ^ flip))


def spread_move(value, k):
    return permute(value, lambda x, y, c: (x + k, y, c) if c == 1 else ((x, y + 2, c) if k != 2 else None))


def on_device(gradient, second_moment, left_root, right_root, block_rows, block_cols, block_owner):
    shard_rows, width = gradient.shape
    cols = width // BS
    fsdp = lax.axis_size("fsdp")
    groups = lax.axis_size("group")
    me = lax.axis_index("fsdp")
    group = lax.axis_index("group")
    quarters = BS // shard_rows
    row_count = fsdp // quarters
    half = shard_rows // 2
    part = half // 4
    place = jnp.stack([me, group]).astype(jnp.int32)
    up = [(i, (i + 1) % groups) for i in range(groups)]
    down = [(i, (i - 1) % groups) for i in range(groups)]
    across = lambda v, w: lax.ppermute(v, "group", w)
    every = lambda v: lax.all_to_all(v, "fsdp", 0, 0, tiled=True)

    h, w = 64, 128
    mixed = gradient[:, :BS].reshape(shard_rows // h, h, BS // w, w).transpose(2, 0, 1, 3)
    spread = every(mixed.reshape(fsdp, h, w))

    give = lax.dynamic_slice(gradient, ((1 - me % 2) * half, BS), (half, BS))
    other = swap_cores(give)
    moment, norm = adam(gradient, second_moment)
    tables = make_tables(block_rows, block_cols, block_owner, place, fsdp, cols, row_count)
    spread_tab, _, fwd, _, back_tab, _, from_tab, offsets, mine, far_tab, row_of, owner_of = tables

    lanes = pl.ds(BS, BS)

    @counted(6)
    def spread_pieces(tab, ins, outs):
        mine_ref, other_ref = ins
        core = tab[0]
        made = []
        for k in (1, 2, 3):
            at = pl.multiple_of(tab[1 + k] * part, part)
            here = pl.multiple_of(core * half + at, part)
            made.append(([(None, mine_ref.at[pl.ds(here, part), lanes])], outs[k - 1].at[core]))
            made.append(([(None, other_ref.at[pl.ds(at, part), :])], outs[k - 1].at[1 - core]))
        return made

    sends = table_mover("spread_send", spread_tab, [gradient, other], [(2, part, BS)] * 3, spread_pieces, (part, BS))
    arrived = {k: spread_move(sends[k - 1], k) for k in (1, 3, 2)}
    arrived = [arrived[k] for k in (1, 2, 3)]

    @counted(8)
    def stack_pieces(tab, ins, outs):
        mine_ref, other_ref, got = ins[0], ins[1], ins[2:]
        core = tab[0]
        made = []
        for k in range(4):
            u = tab[5 + k]
            at = pl.multiple_of(tab[5 + k] * part, part)
            here = pl.multiple_of(core * half + at, part)
            local = (mine_ref.at[pl.ds(here, part), lanes], other_ref.at[pl.ds(at, part), :])
            for e in range(2):
                src_e = core if e == 0 else 1 - core
                if k == 0:
                    choices = [(None, local[e])]
                elif k == 2:
                    choices = [(core == 0, local[e]), (core == 1, got[1].at[src_e])]
                else:
                    choices = [(None, got[k - 1].at[src_e])]
                made.append((choices, outs[0].at[u, src_e]))
        return made

    (stacked,) = table_mover(
        "spread_stack", spread_tab, [gradient, other, *arrived], [(4, 2, part, BS)], stack_pieces, (part, BS)
    )
    stacked, spread = lax.optimization_barrier((stacked, spread))

    picked0 = pick_for_owners(0, row_of, spread.reshape(row_count, quarters * h, w), norm)
    got = {k: along_first(stacked, k) for k in (1, 3, 2)}
    picked0, got = lax.optimization_barrier((picked0, got))
    got0 = every(picked0)
    picked = picker("to_owners", fwd, [stacked, got[1], got[2], got[3]], 8, 2, (2, part, BS))
    far_pieces = [(0, 1), (0, 3), (1, 1), (1, 3), (0, 2), (1, 2), (1, 0)]
    bufs = {(0, 0): picked[0]}
    for f, k in far_pieces:
        bufs[f, k] = along_second(picked[f * 4 + k], k, f)

    got0, bufs = lax.optimization_barrier((got0, bufs))
    (done0,) = shampoo(0, mine, offsets, got0, left_root, right_root, [got0], (fsdp, quarters * h, w))
    bufs = [bufs[f, k] for f in range(2) for k in range(4)]
    done = shampoo(1, mine, offsets, got0, left_root, right_root, bufs, bufs[0].shape)

    home0 = every(pick_from_owners(0, owner_of, every(done0)).reshape(fsdp, h, w))
    before, after = across(home0, up), across(home0, down)
    far_lo, far_hi = across(before[: fsdp // 2], up), across(after[fsdp // 2 :], down)
    update = column_rows(0, cols, groups, far_tab, [home0, before, after, far_lo, far_hi])

    back = {(0, 0): done[0]}
    for f, k in far_pieces:
        back[f, k] = back_second(done[f * 4 + k], k, f)
    back = [back[f, k] for f in range(2) for k in range(4)]
    replies = picker("to_homes", back_tab, back, 4, 4, (2, part, BS))
    held = {k: along_first(replies[k], k) for k in (1, 3, 2)}
    held = [replies[0]] + [held[k] for k in (1, 2, 3)]
    slots = picker("from_owners", from_tab, held, 4, 1, (2, part, BS))
    arrived = [spread_move(slots[k][0], k) for k in (1, 2, 3)]

    @counted(8)
    def home_pieces(tab, ins, outs):
        core = tab[0]
        made = []
        for k in range(4):
            at = pl.multiple_of(tab[5 + k] * part, part)
            for i, e in enumerate((core, 1 - core)):
                if k == 2:
                    choices = [(core == 0, ins[1].at[0, e]), (core == 1, ins[3].at[e])]
                elif k == 0:
                    choices = [(None, ins[0].at[0, e])]
                else:
                    choices = [(None, ins[1 + k].at[e])]
                made.append((choices, outs[i].at[pl.ds(at, part), :]))
        return made

    keep, give = table_mover(
        "home", spread_tab, [slots[0], slots[2], *arrived], [(half, BS)] * 2, home_pieces, (part, BS)
    )
    got = swap_cores(give)
    k_up, k_down, g_up, g_down = across(keep, up), across(keep, down), across(got, up), across(got, down)
    k_far, g_far = across(k_up, up), across(g_down, down)
    update = whole_rows(
        1, cols, groups, far_tab, [keep, got, k_up, g_up, k_down, g_down, k_far, g_far], update
    )
    return update, moment


def solution(mesh):
    placed = (
        P("fsdp", "group"),
        P("fsdp", "group"),
        P("group", "fsdp", None, None, None),
        P("group", "fsdp", None, None, None),
        P(),
        P(),
        P(),
    )
    return jax.shard_map(
        on_device,
        mesh=mesh,
        in_specs=placed,
        out_specs=(P("fsdp", None), P("fsdp", "group")),
        check_vma=False,
    )
```

time: 687 us -> 233 us (0.34)
  blocking collectives: 457 us -> 0 us
  starting transfers between devices: 8.96 us -> 109 us
  matrix products: 76.5 us -> 0 us
  local copies, waits for them, and re-layouts: 71.5 us -> 4.82 us
  Pallas kernels: 0 us -> 52.9 us
  waiting for transfers between devices: 47.2 us -> 64.1 us
  between operations: 14.6 us -> 1.31 us
    psum x1 -> x0, blocking collectives: 254 us -> none  [on_device(): adam_sq = lax.psum(local_table, 'fsdp')]
    all_to_all x1 -> x0, blocking collectives: 203 us -> none  [on_device(): lax.all_to_all(replies, 'fsdp', split_axis=0, concat_axis=0, tiled=True)]
    dot_general x6 -> x0, matrix products: 76.5 us -> none  [the longest x1 31.2 us: on_device(): jnp.einsum('sij,sjk->sik', left_product, right_slots, precision=highest)]
    ppermute x0 -> x38, starting transfers between devices: none -> 66.3 us  [the longest x28 48.2 us: permute(): return lax.ppermute(value, 'fsdp', pairs)]
    ppermute x0 -> x38, waiting for transfers between devices: none -> 61.3 us  [the longest x28 42.7 us: permute(): return lax.ppermute(value, 'fsdp', pairs)]
    pallas_call x0 -> x14, Pallas kernels: none -> 52.9 us  [the longest x2 20.5 us: shampoo(): pl.pallas_call(functools.partial(shampoo_kernel, b, len(bufs)), in_specs=...]
    all_gather x1 -> x0, waiting for transfers between devices: 47.2 us -> none  [on_device(): update = lax.all_gather(own_update, 'group', axis=1, tiled=True)]
    convert_element_type x2 -> x0, local copies, waits for them, and re-layouts: 41.4 us -> none  [the longest x1 20.7 us: on_device(): outgoing = jnp.einsum('dc,rcb->drb', choose_dest, gradient.reshape(shard_...]
  transfers between devices with their start and end apart: 2 -> 42, of which waited for: 1 -> 18; matrix products, arithmetic and copies ran while one was open for 1% -> 0% of each run, Pallas kernels for 0% -> 21%
where the time goes in v2:
time: 233 us
  starting transfers between devices  109 us (47%)
  waiting for transfers between devices  64.1 us (28%)
  Pallas kernels  52.9 us (23%)
  local copies, waits for them, and re-layouts  4.82 us (2%)
    ppermute x28, starting transfers between devices, permute(): return lax.ppermute(value, 'fsdp', pairs)  48.2 us
    all_to_all x4, starting transfers between devices, on_device(): every = lambda v: lax.all_to_all(v, 'fsdp', 0, 0, tiled=True)  42.7 us
    ppermute x28, waiting for transfers between devices, permute(): return lax.ppermute(value, 'fsdp', pairs)  42.7 us
    pallas_call x2, Pallas kernels, shampoo(): pl.pallas_call(functools.partial(shampoo_kernel, b, len(bufs)), in_specs=...  20.5 us
    ppermute x10, waiting for transfers between devices, on_device(): across = lambda v, w: lax.ppermute(v, 'group', w)  18.5 us
    ppermute x10, starting transfers between devices, on_device(): across = lambda v, w: lax.ppermute(v, 'group', w)  18.1 us
    pallas_call x3, Pallas kernels, picker(): pl.pallas_call(kernel, in_specs=[SMEM] + [ANY] * (n_in + len(before)), ou...  9.18 us
    pallas_call x3, Pallas kernels, table_mover(): pl.pallas_call(kernel, in_specs=[SMEM] + [ANY] * n_in, out_specs=[ANY] *...  5.6 us
  transfers between devices with their start and end apart: 42, of which 18 were waited for; matrix products, arithmetic and copies ran while one was open for 0% of the time, Pallas kernels for 21%

profile of v2, /device:TPU:1, one launch (start us, length us, event | category | flops | bytes accessed | tf_op | source)
XLA Modules:
  0.0 232.7 jit_solution(10012454451631367996)
XLA Ops:
  2.8 8.6 %all-to-all-start = ((bf16[32,64,128]{2,1,0:T(8,128)(2,1)}), bf16[32,64,128]{2,1,0:T(8,128)(2,1)S(1)}, u32[]{:S(2)}, u32[]{:S(2)}) async-start(bf16[32,64,128]{2,1,0:T(8,128)(2,1)} %bitcast.3), calls=%async_computation | async-start | bytes 1048576 | tf_op jit(solution)/shard_map/all_to_all | solution.py:585
  12.3 3.0 %tables.1 = (s32[9]{0:T(128)}, s32[2,16]{1,0:T(2,128)}, s32[2,16]{1,0:T(2,128)}, s32[2,16]{1,0:T(2,128)}, s32[2,16]{1,0:T(2,128)}, /*index=5*/s32[2,4]{1,0:T(2,1...) custom-call(s32[4,16]{1,0:T(4,128)} %rows_ref.1, ...), custom_call_target="tpu_custom_call" | custom-call | tf_op jit(solution)/shard_map/tables/pallas_call | solution.py:158
  19.0 4.3 %collective-permute-start.2 = (bf16[2,32,1024]{2,1,0:T(8,128)(2,1)S(1)}, bf16[2,32,1024]{2,1,0:T(8,128)(2,1)S(1)}, u32[]{:S(2)}, u32[]{:S(2)}) collective-permute-start(bf16[2,32,1024]{2,1,0:T(8,128)(2,1)S(1)} %get-tuple-element.65), channel_id=1, source_target_pairs={{1,17},{3,19},{5,21},{7,23},{9,25},{11,27},{13,29},{15,31},{17,1},... | collective-permute-start | bytes 393224 | tf_op jit(solution)/shard_map/ppermute | solution.py:547
  33.6 4.6 %adam.1 = (f32[256,2048]{1,0:T(8,128)}, bf16[16,128]{1,0:T(8,128)(2,1)}) custom-call(bf16[256,2048]{1,0:T(8,128)(2,1)} %g_ref.1, f32[256,2048]{1,0:T(8,128)} %m_ref.1), custom_call_target="tpu_custom_call" | custom-call | tf_op jit(solution)/shard_map/adam/pallas_call | solution.py:58
  44.2 3.7 %collective-permute-done.4.refs_1_ = bf16[4,2,32,1024]{3,2,1,0:T(8,128)(2,1)S(1)} collective-permute-done((bf16[4,2,32,1024]{3,2,1,0:T(8,128)(2,1)S(1)}, bf16[4,2,32,1024]{3,2,1,0:T(8,128)(2,1)S(1)}, u32[]{:S(2)}, u32[]{:S(2)}) %collective-permute-start.4) | collective-permute-done | bytes 524320 | tf_op jit(solution)/shard_map/ppermute | solution.py:547
  47.9 6.4 %all-to-all-start.1 = ((bf16[32,272,128]{2,1,0:T(8,128)(2,1)}), bf16[32,272,128]{2,1,0:T(8,128)(2,1)}, u32[]{:S(2)}, u32[]{:S(2)}) async-start(bf16[32,272,128]{2,1,0:T(8,128)(2,1)} %pick_for_owners.1), calls=%async_computation.1 | async-start | bytes 4456448 | tf_op jit(solution)/shard_map/all_to_all | solution.py:585
  54.3 4.0 %to_owners.1 = (bf16[2,2,32,1024]{3,2,1,0:T(8,128)(2,1)S(1)}, bf16[2,2,32,1024]{3,2,1,0:T(8,128)(2,1)S(1)}, bf16[2,2,32,1024]{3,2,1,0:T(8,128)(2,1)S(1)}, bf16[2...) custom-call(s32[2,16]{1,0:T(2,128)S(1)} %copy-done.11, ...), custom_call_target="tpu_custom_call" | custom-call | bytes 4194304 | tf_op jit(solution)/shard_map/to_owners/pallas_call | solution.py:249
  65.7 19.2 %collective-permute-done.7.refs_1_ = bf16[2,2,32,1024]{3,2,1,0:T(8,128)(2,1)S(1)} collective-permute-done((bf16[2,2,32,1024]{3,2,1,0:T(8,128)(2,1)S(1)}, bf16[2,2,32,1024]{3,2,1,0:T(8,128)(2,1)S(1)}, u32[]{:S(2)}, u32[]{:S(2)}) %collective-permute-start.7) | collective-permute-done | bytes 262176 | tf_op jit(solution)/shard_map/ppermute | solution.py:547
  84.9 3.1 %collective-permute-start.12 = (bf16[2,2,32,1024]{3,2,1,0:T(8,128)(2,1)S(1)}, bf16[2,2,32,1024]{3,2,1,0:T(8,128)(2,1)S(1)}, u32[]{:S(2)}, u32[]{:S(2)}) collective-permute-start(bf16[2,2,32,1024]{3,2,1,0:T(8,128)(2,1)S(1)} %get-tuple-element.81), channel_id=1, source_target_pairs={{0,5},{1,16},{2,7},{3,18},{4,1},{5,20},{6,3},{7,22},{8,13},{9,24},... | collective-permute-start | bytes 786440 | tf_op jit(solution)/shard_map/ppermute | solution.py:547
  96.7 21.6 %all-to-all-start.2 = ((bf16[32,256,128]{2,1,0:T(8,128)(2,1)}), bf16[32,256,128]{2,1,0:T(8,128)(2,1)S(1)}, u32[]{:S(2)}, u32[]{:S(2)}) async-start(bf16[32,256,128]{2,1,0:T(8,128)(2,1)} %shampoo.3), calls=%async_computation.2 | async-start | bytes 4194304 | tf_op jit(solution)/shard_map/all_to_all | solution.py:585
  118.3 19.1 %shampoo.2 = (bf16[2,2,32,1024]{3,2,1,0:T(8,128)(2,1)}, bf16[2,2,32,1024]{3,2,1,0:T(8,128)(2,1)}, bf16[2,2,32,1024]{3,2,1,0:T(8,128)(2,1)}, bf16[2,2,32,1024]{3,...) custom-call(s32[3,2]{1,0:T(4,128)} %get-tuple-element.61.mine_ref, ...), custom_call_target="tpu_custom_call" | custom-call | flops 10737418240 | bytes 12582912 | tf_op jit(solution)/shard_map/shampoo/pallas_call | solution.py:374
  137.6 3.2 %collective-permute-start.15 = (bf16[2,2,32,1024]{3,2,1,0:T(8,128)(2,1)}, bf16[2,2,32,1024]{3,2,1,0:T(8,128)(2,1)S(1)}, u32[]{:S(2)}, u32[]{:S(2)}) collective-permute-start(bf16[2,2,32,1024]{3,2,1,0:T(8,128)(2,1)} %get-tuple-element.94), channel_id=1, source_target_pairs={{0,4},{1,17},{2,6},{3,19},{4,0},{5,21},{6,2},{7,23},{8,12},{9,25},... | collective-permute-start | bytes 786440 | tf_op jit(solution)/shard_map/ppermute | solution.py:547
  144.0 3.3 %collective-permute-done.14.refs_1_ = bf16[2,2,32,1024]{3,2,1,0:T(8,128)(2,1)S(1)} collective-permute-done((bf16[2,2,32,1024]{3,2,1,0:T(8,128)(2,1)}, bf16[2,2,32,1024]{3,2,1,0:T(8,128)(2,1)S(1)}, u32[]{:S(2)}, u32[]{:S(2)}) %collective-permute-start.14) | collective-permute-done | bytes 262176 | tf_op jit(solution)/shard_map/ppermute | solution.py:547
  147.3 4.4 %collective-permute-start.19 = (bf16[2,2,32,1024]{3,2,1,0:T(8,128)(2,1)}, bf16[2,2,32,1024]{3,2,1,0:T(8,128)(2,1)}, u32[]{:S(2)}, u32[]{:S(2)}) collective-permute-start(bf16[2,2,32,1024]{3,2,1,0:T(8,128)(2,1)} %get-tuple-element.98), channel_id=1, source_target_pairs={{0,17},{1,4},{2,19},{3,6},{4,21},{5,0},{6,23},{7,2},{8,25},{9,12},... | collective-permute-start | bytes 786440 | tf_op jit(solution)/shard_map/ppermute | solution.py:547
  151.6 3.0 %collective-permute-start.20 = (bf16[2,2,32,1024]{3,2,1,0:T(8,128)(2,1)}, bf16[2,2,32,1024]{3,2,1,0:T(8,128)(2,1)}, u32[]{:S(2)}, u32[]{:S(2)}) collective-permute-start(bf16[2,2,32,1024]{3,2,1,0:T(8,128)(2,1)} %get-tuple-element.99), channel_id=1, source_target_pairs={{0,9},{1,2},{2,11},{3,4},{4,13},{5,6},{6,15},{7,0},{8,17},{9,10},{... | collective-permute-start | bytes 786440 | tf_op jit(solution)/shard_map/ppermute | solution.py:547
  156.8 6.2 %all-to-all-start.3 = ((bf16[32,64,128]{2,1,0:T(8,128)(2,1)}), bf16[32,64,128]{2,1,0:T(8,128)(2,1)S(1)}, u32[]{:S(2)}, u32[]{:S(2)}) async-start(bf16[32,64,128]{2,1,0:T(8,128)(2,1)} %bitcast.8), calls=%async_computation.3 | async-start | bytes 1048576 | tf_op jit(solution)/shard_map/all_to_all | solution.py:585
  163.1 3.7 %to_homes.1 = (bf16[4,2,32,1024]{3,2,1,0:T(8,128)(2,1)S(1)}, bf16[4,2,32,1024]{3,2,1,0:T(8,128)(2,1)}, bf16[4,2,32,1024]{3,2,1,0:T(8,128)(2,1)}, bf16[4,2,32,1024]{3,2,1,0:T(8,128)(2,1)}) custom-call(s32[2,16]{1,0:T(2,128)S(1)} %copy-done.10, bf16[2,2,32,1024]{3,2,1,0:T(8,128)(2,1)S(1)} %copy-done.1, ...), custom_call_target="tpu_custom_call" | custom-call | bytes 4194304 | tf_op jit(solution)/shard_map/to_homes/pallas_call | solution.py:249
  174.7 5.1 %collective-permute-start.35 = (bf16[32,64,128]{2,1,0:T(8,128)(2,1)S(1)}, bf16[32,64,128]{2,1,0:T(8,128)(2,1)S(1)}, u32[]{:S(2)}, u32[]{:S(2)}) collective-permute-start(bf16[32,64,128]{2,1,0:T(8,128)(2,1)S(1)} %all-to-all-done.3.own), channel_id=1, source_target_pairs={{0,96},{32,0},{64,32},{96,64},{1,97},{33,1},{65,33},{97,65},{2,98}... | collective-permute-start | bytes 1572872 | tf_op jit(solution)/shard_map/ppermute | solution.py:584
  179.8 5.1 %collective-permute-done.22.refs_2_ = bf16[4,2,32,1024]{3,2,1,0:T(8,128)(2,1)S(1)} collective-permute-done((bf16[4,2,32,1024]{3,2,1,0:T(8,128)(2,1)}, bf16[4,2,32,1024]{3,2,1,0:T(8,128)(2,1)S(1)}, u32[]{:S(2)}, u32[]{:S(2)}) %collective-permute-start.22) | collective-permute-done | bytes 524320 | tf_op jit(solution)/shard_map/ppermute | solution.py:547
  200.9 4.2 %collective-permute-start.31 = (bf16[128,1024]{1,0:T(8,128)(2,1)S(1)}, bf16[128,1024]{1,0:T(8,128)(2,1)S(1)}, u32[]{:S(2)}, u32[]{:S(2)}) collective-permute-start(bf16[128,1024]{1,0:T(8,128)(2,1)S(1)} %collective-permute-done.27.refs_1_), channel_id=1, source_target_pairs={{0,96},{32,0},{64,32},{96,64},{1,97},{33,1},{65,33},{97,65},{2,98}... | collective-permute-start | bytes 786440 | tf_op jit(solution)/shard_map/ppermute | solution.py:584
  205.3 3.8 %collective-permute-done.34.before = bf16[32,64,128]{2,1,0:T(8,128)(2,1)S(1)} collective-permute-done((bf16[32,64,128]{2,1,0:T(8,128)(2,1)S(1)}, bf16[32,64,128]{2,1,0:T(8,128)(2,1)S(1)}, u32[]{:S(2)}, u32[]{:S(2)}) %collective-permute-start.34) | collective-permute-done | bytes 524320 | tf_op jit(solution)/shard_map/ppermute | solution.py:584
  209.2 5.5 %collective-permute-done.28.refs_2_ = bf16[128,1024]{1,0:T(8,128)(2,1)S(1)} collective-permute-done((bf16[128,1024]{1,0:T(8,128)(2,1)S(1)}, bf16[128,1024]{1,0:T(8,128)(2,1)S(1)}, u32[]{:S(2)}, u32[]{:S(2)}) %collective-permute-start.28) | collective-permute-done | bytes 262176 | tf_op jit(solution)/shard_map/ppermute | solution.py:584
  216.3 3.4 %collective-permute-start.33 = (bf16[128,1024]{1,0:T(8,128)(2,1)S(1)}, bf16[128,1024]{1,0:T(8,128)(2,1)S(1)}, u32[]{:S(2)}, u32[]{:S(2)}) collective-permute-start(bf16[128,1024]{1,0:T(8,128)(2,1)S(1)} %collective-permute-done.31.refs_5_), channel_id=1, source_target_pairs={{0,96},{32,0},{64,32},{96,64},{1,97},{33,1},{65,33},{97,65},{2,98}... | collective-permute-start | bytes 786440 | tf_op jit(solution)/shard_map/ppermute | solution.py:584
  225.9 4.5 %collective-permute-done.32.refs_6_ = bf16[128,1024]{1,0:T(8,128)(2,1)S(1)} collective-permute-done((bf16[128,1024]{1,0:T(8,128)(2,1)S(1)}, bf16[128,1024]{1,0:T(8,128)(2,1)S(1)}, u32[]{:S(2)}, u32[]{:S(2)}) %collective-permute-start.32) | collective-permute-done | bytes 262176 | tf_op jit(solution)/shard_map/ppermute | solution.py:584
  (120 shorter events, 78.6 us)
Async XLA Ops:
  2.8 27.4 %all-to-all-start = ((bf16[32,64,128]{2,1,0:T(8,128)(2,1)}), bf16[32,64,128]{2,1,0:T(8,128)(2,1)S(1)}, u32[]{:S(2)}, u32[]{:S(2)}) async-start(bf16[32,64,128]{2,1,0:T(8,128)(2,1)} %bitcast.3), calls=%async_computation | async-start | bytes 1048576 | tf_op jit(solution)/shard_map/all_to_all | solution.py:585
  30.2 14.0 %collective-permute-start.6 = (bf16[4,2,32,1024]{3,2,1,0:T(8,128)(2,1)S(1)}, bf16[4,2,32,1024]{3,2,1,0:T(8,128)(2,1)S(1)}, u32[]{:S(2)}, u32[]{:S(2)}) collective-permute-start(bf16[4,2,32,1024]{3,2,1,0:T(8,128)(2,1)S(1)} %spread_stack.1.refs_0_), channel_id=1, source_target_pairs={{0,24},{1,7},{2,26},{3,1},{4,28},{5,3},{6,30},{7,5},{8,0},{9,15},{... | collective-permute-start | bytes 1572872 | tf_op jit(solution)/shard_map/ppermute | solution.py:547
  33.0 14.9 %collective-permute-start.4 = (bf16[4,2,32,1024]{3,2,1,0:T(8,128)(2,1)S(1)}, bf16[4,2,32,1024]{3,2,1,0:T(8,128)(2,1)S(1)}, u32[]{:S(2)}, u32[]{:S(2)}) collective-permute-start(bf16[4,2,32,1024]{3,2,1,0:T(8,128)(2,1)S(1)} %spread_stack.1.refs_0_), channel_id=1, source_target_pairs={{0,8},{1,3},{2,10},{3,5},{4,12},{5,7},{6,14},{7,1},{8,16},{9,11},{... | collective-permute-start | bytes 1572872 | tf_op jit(solution)/shard_map/ppermute | solution.py:547
  47.9 47.4 %all-to-all-start.1 = ((bf16[32,272,128]{2,1,0:T(8,128)(2,1)}), bf16[32,272,128]{2,1,0:T(8,128)(2,1)}, u32[]{:S(2)}, u32[]{:S(2)}) async-start(bf16[32,272,128]{2,1,0:T(8,128)(2,1)} %pick_for_owners.1), calls=%async_computation.1 | async-start | bytes 4456448 | tf_op jit(solution)/shard_map/all_to_all | solution.py:585
  58.3 26.6 %collective-permute-start.7 = (bf16[2,2,32,1024]{3,2,1,0:T(8,128)(2,1)S(1)}, bf16[2,2,32,1024]{3,2,1,0:T(8,128)(2,1)S(1)}, u32[]{:S(2)}, u32[]{:S(2)}) collective-permute-start(bf16[2,2,32,1024]{3,2,1,0:T(8,128)(2,1)S(1)} %get-tuple-element.76), channel_id=1, source_target_pairs={{0,2},{1,9},{2,4},{3,11},{4,6},{5,13},{6,0},{7,15},{8,10},{9,17},{... | collective-permute-start | bytes 786440 | tf_op jit(solution)/shard_map/ppermute | solution.py:547
  59.8 28.4 %collective-permute-start.8 = (bf16[2,2,32,1024]{3,2,1,0:T(8,128)(2,1)S(1)}, bf16[2,2,32,1024]{3,2,1,0:T(8,128)(2,1)S(1)}, u32[]{:S(2)}, u32[]{:S(2)}) collective-permute-start(bf16[2,2,32,1024]{3,2,1,0:T(8,128)(2,1)S(1)} %get-tuple-element.77), channel_id=1, source_target_pairs={{0,4},{1,17},{2,6},{3,19},{4,0},{5,21},{6,2},{7,23},{8,12},{9,25},... | collective-permute-start | bytes 786440 | tf_op jit(solution)/shard_map/ppermute | solution.py:547
  62.3 28.8 %collective-permute-start.9 = (bf16[2,2,32,1024]{3,2,1,0:T(8,128)(2,1)S(1)}, bf16[2,2,32,1024]{3,2,1,0:T(8,128)(2,1)S(1)}, u32[]{:S(2)}, u32[]{:S(2)}) collective-permute-start(bf16[2,2,32,1024]{3,2,1,0:T(8,128)(2,1)S(1)} %get-tuple-element.78), channel_id=1, source_target_pairs={{0,6},{1,25},{2,0},{3,27},{4,2},{5,29},{6,4},{7,31},{8,14},{9,1},{... | collective-permute-start | bytes 786440 | tf_op jit(solution)/shard_map/ppermute | solution.py:547
  63.4 27.7 %collective-permute-start.10 = (bf16[2,2,32,1024]{3,2,1,0:T(8,128)(2,1)S(1)}, bf16[2,2,32,1024]{3,2,1,0:T(8,128)(2,1)S(1)}, u32[]{:S(2)}, u32[]{:S(2)}) collective-permute-start(bf16[2,2,32,1024]{3,2,1,0:T(8,128)(2,1)S(1)} %get-tuple-element.79), channel_id=1, source_target_pairs={{0,1},{1,0},{2,3},{3,2},{4,5},{5,4},{6,7},{7,6},{8,9},{9,8},{10,11... | collective-permute-start | bytes 786440 | tf_op jit(solution)/shard_map/ppermute | solution.py:547
  64.6 26.6 %collective-permute-start.11 = (bf16[2,2,32,1024]{3,2,1,0:T(8,128)(2,1)S(1)}, bf16[2,2,32,1024]{3,2,1,0:T(8,128)(2,1)S(1)}, u32[]{:S(2)}, u32[]{:S(2)}) collective-permute-start(bf16[2,2,32,1024]{3,2,1,0:T(8,128)(2,1)S(1)} %get-tuple-element.80), channel_id=1, source_target_pairs={{0,3},{1,8},{2,5},{3,10},{4,7},{5,12},{6,1},{7,14},{8,11},{9,16},{... | collective-permute-start | bytes 786440 | tf_op jit(solution)/shard_map/ppermute | solution.py:547
  96.7 57.9 %all-to-all-start.2 = ((bf16[32,256,128]{2,1,0:T(8,128)(2,1)}), bf16[32,256,128]{2,1,0:T(8,128)(2,1)S(1)}, u32[]{:S(2)}, u32[]{:S(2)}) async-start(bf16[32,256,128]{2,1,0:T(8,128)(2,1)} %shampoo.3), calls=%async_computation.2 | async-start | bytes 4194304 | tf_op jit(solution)/shard_map/all_to_all | solution.py:585
  137.6 14.1 %collective-permute-start.15 = (bf16[2,2,32,1024]{3,2,1,0:T(8,128)(2,1)}, bf16[2,2,32,1024]{3,2,1,0:T(8,128)(2,1)S(1)}, u32[]{:S(2)}, u32[]{:S(2)}) collective-permute-start(bf16[2,2,32,1024]{3,2,1,0:T(8,128)(2,1)} %get-tuple-element.94), channel_id=1, source_target_pairs={{0,4},{1,17},{2,6},{3,19},{4,0},{5,21},{6,2},{7,23},{8,12},{9,25},... | collective-permute-start | bytes 786440 | tf_op jit(solution)/shard_map/ppermute | solution.py:547
  140.7 22.3 %collective-permute-start.16 = (bf16[2,2,32,1024]{3,2,1,0:T(8,128)(2,1)}, bf16[2,2,32,1024]{3,2,1,0:T(8,128)(2,1)S(1)}, u32[]{:S(2)}, u32[]{:S(2)}) collective-permute-start(bf16[2,2,32,1024]{3,2,1,0:T(8,128)(2,1)} %get-tuple-element.95), channel_id=1, source_target_pairs={{0,2},{1,9},{2,4},{3,11},{4,6},{5,13},{6,0},{7,15},{8,10},{9,17},{... | collective-permute-start | bytes 786440 | tf_op jit(solution)/shard_map/ppermute | solution.py:547
  141.3 21.7 %collective-permute-start.17 = (bf16[2,2,32,1024]{3,2,1,0:T(8,128)(2,1)}, bf16[2,2,32,1024]{3,2,1,0:T(8,128)(2,1)S(1)}, u32[]{:S(2)}, u32[]{:S(2)}) collective-permute-start(bf16[2,2,32,1024]{3,2,1,0:T(8,128)(2,1)} %get-tuple-element.96), channel_id=1, source_target_pairs={{0,1},{1,0},{2,3},{3,2},{4,5},{5,4},{6,7},{7,6},{8,9},{9,8},{10,11... | collective-permute-start | bytes 786440 | tf_op jit(solution)/shard_map/ppermute | solution.py:547
  142.5 20.5 %collective-permute-start.18 = (bf16[2,2,32,1024]{3,2,1,0:T(8,128)(2,1)}, bf16[2,2,32,1024]{3,2,1,0:T(8,128)(2,1)}, u32[]{:S(2)}, u32[]{:S(2)}) collective-permute-start(bf16[2,2,32,1024]{3,2,1,0:T(8,128)(2,1)} %get-tuple-element.97), channel_id=1, source_target_pairs={{0,25},{1,6},{2,27},{3,0},{4,29},{5,2},{6,31},{7,4},{8,1},{9,14},{... | collective-permute-start | bytes 786440 | tf_op jit(solution)/shard_map/ppermute | solution.py:547
  147.3 15.7 %collective-permute-start.19 = (bf16[2,2,32,1024]{3,2,1,0:T(8,128)(2,1)}, bf16[2,2,32,1024]{3,2,1,0:T(8,128)(2,1)}, u32[]{:S(2)}, u32[]{:S(2)}) collective-permute-start(bf16[2,2,32,1024]{3,2,1,0:T(8,128)(2,1)} %get-tuple-element.98), channel_id=1, source_target_pairs={{0,17},{1,4},{2,19},{3,6},{4,21},{5,0},{6,23},{7,2},{8,25},{9,12},... | collective-permute-start | bytes 786440 | tf_op jit(solution)/shard_map/ppermute | solution.py:547
  156.8 17.9 %all-to-all-start.3 = ((bf16[32,64,128]{2,1,0:T(8,128)(2,1)}), bf16[32,64,128]{2,1,0:T(8,128)(2,1)S(1)}, u32[]{:S(2)}, u32[]{:S(2)}) async-start(bf16[32,64,128]{2,1,0:T(8,128)(2,1)} %bitcast.8), calls=%async_computation.3 | async-start | bytes 1048576 | tf_op jit(solution)/shard_map/all_to_all | solution.py:585
  168.3 16.6 %collective-permute-start.22 = (bf16[4,2,32,1024]{3,2,1,0:T(8,128)(2,1)}, bf16[4,2,32,1024]{3,2,1,0:T(8,128)(2,1)S(1)}, u32[]{:S(2)}, u32[]{:S(2)}) collective-permute-start(bf16[4,2,32,1024]{3,2,1,0:T(8,128)(2,1)} %get-tuple-element.102), channel_id=1, source_target_pairs={{0,16},{1,5},{2,18},{3,7},{4,20},{5,1},{6,22},{7,3},{8,24},{9,13},... | collective-permute-start | bytes 1572872 | tf_op jit(solution)/shard_map/ppermute | solution.py:547
  170.7 14.2 %collective-permute-start.23 = (bf16[4,2,32,1024]{3,2,1,0:T(8,128)(2,1)}, bf16[4,2,32,1024]{3,2,1,0:T(8,128)(2,1)S(1)}, u32[]{:S(2)}, u32[]{:S(2)}) collective-permute-start(bf16[4,2,32,1024]{3,2,1,0:T(8,128)(2,1)} %get-tuple-element.103), channel_id=1, source_target_pairs={{0,24},{1,7},{2,26},{3,1},{4,28},{5,3},{6,30},{7,5},{8,0},{9,15},{... | collective-permute-start | bytes 1572872 | tf_op jit(solution)/shard_map/ppermute | solution.py:547
  174.7 30.5 %collective-permute-start.35 = (bf16[32,64,128]{2,1,0:T(8,128)(2,1)S(1)}, bf16[32,64,128]{2,1,0:T(8,128)(2,1)S(1)}, u32[]{:S(2)}, u32[]{:S(2)}) collective-permute-start(bf16[32,64,128]{2,1,0:T(8,128)(2,1)S(1)} %all-to-all-done.3.own), channel_id=1, source_target_pairs={{0,96},{32,0},{64,32},{96,64},{1,97},{33,1},{65,33},{97,65},{2,98}... | collective-permute-start | bytes 1572872 | tf_op jit(solution)/shard_map/ppermute | solution.py:584
  191.4 17.7 %collective-permute-start.34 = (bf16[32,64,128]{2,1,0:T(8,128)(2,1)S(1)}, bf16[32,64,128]{2,1,0:T(8,128)(2,1)S(1)}, u32[]{:S(2)}, u32[]{:S(2)}) collective-permute-start(bf16[32,64,128]{2,1,0:T(8,128)(2,1)S(1)} %all-to-all-done.3.own), channel_id=1, source_target_pairs={{0,32},{32,64},{64,96},{96,0},{1,33},{33,65},{65,97},{97,1},{2,34}... | collective-permute-start | bytes 1572872 | tf_op jit(solution)/shard_map/ppermute | solution.py:584
  198.5 16.2 %collective-permute-start.28 = (bf16[128,1024]{1,0:T(8,128)(2,1)S(1)}, bf16[128,1024]{1,0:T(8,128)(2,1)S(1)}, u32[]{:S(2)}, u32[]{:S(2)}) collective-permute-start(bf16[128,1024]{1,0:T(8,128)(2,1)S(1)} %get-tuple-element.108.refs_0_), channel_id=1, source_target_pairs={{0,32},{32,64},{64,96},{96,0},{1,33},{33,65},{65,97},{97,1},{2,34}... | collective-permute-start | bytes 786440 | tf_op jit(solution)/shard_map/ppermute | solution.py:584
  205.2 17.9 %collective-permute-start.30 = (bf16[128,1024]{1,0:T(8,128)(2,1)S(1)}, bf16[128,1024]{1,0:T(8,128)(2,1)S(1)}, u32[]{:S(2)}, u32[]{:S(2)}) collective-permute-start(bf16[128,1024]{1,0:T(8,128)(2,1)S(1)} %get-tuple-element.108.refs_0_), channel_id=1, source_target_pairs={{0,96},{32,0},{64,32},{96,64},{1,97},{33,1},{65,33},{97,65},{2,98}... | collective-permute-start | bytes 786440 | tf_op jit(solution)/shard_map/ppermute | solution.py:584
  214.7 15.7 %collective-permute-start.32 = (bf16[128,1024]{1,0:T(8,128)(2,1)S(1)}, bf16[128,1024]{1,0:T(8,128)(2,1)S(1)}, u32[]{:S(2)}, u32[]{:S(2)}) collective-permute-start(bf16[128,1024]{1,0:T(8,128)(2,1)S(1)} %collective-permute-done.28.refs_2_), channel_id=1, source_target_pairs={{0,32},{32,64},{64,96},{96,0},{1,33},{33,65},{65,97},{97,1},{2,34}... | collective-permute-start | bytes 786440 | tf_op jit(solution)/shard_map/ppermute | solution.py:584
  216.3 14.1 %collective-permute-start.33 = (bf16[128,1024]{1,0:T(8,128)(2,1)S(1)}, bf16[128,1024]{1,0:T(8,128)(2,1)S(1)}, u32[]{:S(2)}, u32[]{:S(2)}) collective-permute-start(bf16[128,1024]{1,0:T(8,128)(2,1)S(1)} %collective-permute-done.31.refs_5_), channel_id=1, source_target_pairs={{0,96},{32,0},{64,32},{96,64},{1,97},{33,1},{65,33},{97,65},{2,98}... | collective-permute-start | bytes 786440 | tf_op jit(solution)/shard_map/ppermute | solution.py:584
  (37 other events, 474.0 us)

commit v3 on v2

--- a/solution.py
+++ b/solution.py
@@ -297,8 +297,8 @@
 
 def shampoo_kernel(b, n_bufs, mine_ref, off_ref, norm_ref, left_ref, right_ref, *refs):
     ins, outs = refs[:n_bufs], refs[n_bufs : 2 * n_bufs]
-    g, lv, rv, rhv, rlv, q, u, acc, norms, g_sem, root_sem, norm_sem, out_sem = refs[2 * n_bufs :]
-    tile = 256
+    g, lv, rv, rhv, rlv, phv, plv, q, u, acc, norms, g_sem, root_sem, norm_sem, out_sem = refs[2 * n_bufs :]
+    tile = 512
     tiles = BS // tile
     slot = mine_ref[0, b]
 
@@ -306,7 +306,9 @@
         rows = pl.ds(pl.multiple_of(t * tile, tile), tile)
         return pltpu.make_async_copy(left_ref.at[0, 0, slot, rows, :], lv.at[rows, :], root_sem.at[t])
 
-    right_load = pltpu.make_async_copy(right_ref.at[0, 0, slot], rv, root_sem.at[tiles])
+    def right_load(t):
+        rows = pl.ds(pl.multiple_of(t * tile, tile), tile)
+        return pltpu.make_async_copy(right_ref.at[0, 0, slot, rows, :], rv.at[rows, :], root_sem.at[tiles + t])
 
     def moves(bufs, box, to_box, sem):
         if n_bufs == 1:
@@ -322,37 +324,34 @@
         left_load(0).start()
         for c in grads:
             c.start()
-        for t in range(1, tiles):
-            left_load(t).start()
-        right_load.start()
+        for t in range(tiles):
+            if t > 0:
+                left_load(t).start()
+            right_load(t).start()
         norm_load.start()
         for c in grads:
             c.wait()
         acc[...] = jnp.zeros_like(acc)
 
-        def step(t, carry):
+        def first(t, carry):
             rows = pl.ds(pl.multiple_of(t * tile, tile), tile)
             left_load(t).wait()
+            right_load(t).wait()
             lh, ll = halves(lv[rows, :])
-            ph, plow = halves(dot(lh, g[...]) + dot(ll, g[...]))
-
-            @pl.when(t == 0)
-            def _():
-                right_load.wait()
-
-                def split(i, carry):
-                    part = pl.ds(pl.multiple_of(i * 128, 128), 128)
-                    rhv[part, :], rlv[part, :] = halves(rv[part, :])
-                    return carry
-
-                lax.fori_loop(0, BS // 128, split, 0)
-
+            rhv[rows, :], rlv[rows, :] = halves(rv[rows, :])
+            phv[rows, :], plv[rows, :] = halves(dot(lh, g[...]) + dot(ll, g[...]))
+            return carry
+
+        def second(t, carry):
+            rows = pl.ds(pl.multiple_of(t * tile, tile), tile)
+            ph, plow = phv[rows, :], plv[rows, :]
             qt = dot(ph, rhv[...]) + (dot(ph, rlv[...]) + dot(plow, rhv[...]))
             q[rows, :] = qt
             acc[...] += jnp.sum((qt * qt).reshape(-1, 8, BS), axis=0)
             return carry
 
-        lax.fori_loop(0, tiles, step, 0)
+        lax.fori_loop(0, tiles, first, 0, unroll=True)
+        lax.fori_loop(0, tiles, second, 0, unroll=True)
         norm_load.wait()
         device = lax.broadcasted_iota(jnp.int32, norms.shape, 0)
         lane = lax.broadcasted_iota(jnp.int32, norms.shape, 2)
@@ -380,6 +379,8 @@
             pltpu.VMEM(big, jnp.bfloat16),
             pltpu.VMEM(big, jnp.float32),
             pltpu.VMEM(big, jnp.float32),
+            pltpu.VMEM(big, jnp.bfloat16),
+            pltpu.VMEM(big, jnp.bfloat16),
             pltpu.VMEM(big, jnp.bfloat16),
             pltpu.VMEM(big, jnp.bfloat16),
             pltpu.VMEM(big, jnp.float32),
@@ -648,9 +649,10 @@
     for f, k in far_pieces:
         bufs[f, k] = along_second(picked[f * 4 + k], k, f)
 
-    got0, bufs = lax.optimization_barrier((got0, bufs))
+    got0, picked_first = lax.optimization_barrier((got0, picked[7]))
     (done0,) = shampoo(0, mine, offsets, got0, left_root, right_root, [got0], (fsdp, quarters * h, w))
     bufs = [bufs[f, k] for f in range(2) for k in range(4)]
+    done0, bufs = lax.optimization_barrier((done0, bufs))
     done = shampoo(1, mine, offsets, got0, left_root, right_root, bufs, bufs[0].shape)
 
     home0 = every(pick_from_owners(0, owner_of, every(done0)).reshape(fsdp, h, w))

time: 233 us -> 226 us (0.970)
  starting transfers between devices: 109 us -> 103 us
  Pallas kernels: 52.9 us -> 50.2 us
    all_to_all x4, waiting for transfers between devices: 2.83 us -> 21.7 us  [on_device(): every = lambda v: lax.all_to_all(v, 'fsdp', 0, 0, tiled=True)]
    all_to_all x4, starting transfers between devices: 42.7 us -> 25.4 us  [on_device(): every = lambda v: lax.all_to_all(v, 'fsdp', 0, 0, tiled=True)]
    ppermute x28, waiting for transfers between devices: 42.7 us -> 27.8 us  [permute(): return lax.ppermute(value, 'fsdp', pairs)]
    ppermute x28, starting transfers between devices: 48.2 us -> 61.4 us  [permute(): return lax.ppermute(value, 'fsdp', pairs)]
    ppermute x10, waiting for transfers between devices: 18.5 us -> 15.3 us  [on_device(): across = lambda v, w: lax.ppermute(v, 'group', w)]
  transfers between devices with their start and end apart: 42 -> 42, of which waited for: 18 -> 17; matrix products, arithmetic and copies ran while one was open for 0% -> 0% of each run, Pallas kernels for 21% -> 21%
where the time goes in v3:
time: 226 us; the launch traced here: 225 us
  starting transfers between devices  103 us (46%)
  waiting for transfers between devices  64.8 us (29%)
  Pallas kernels  50.2 us (22%)
  local copies, waits for them, and re-layouts  5.23 us (2%)
    ppermute x28, starting transfers between devices, permute(): return lax.ppermute(value, 'fsdp', pairs)  61.4 us
    ppermute x28, waiting for transfers between devices, permute(): return lax.ppermute(value, 'fsdp', pairs)  27.8 us
    all_to_all x4, starting transfers between devices, on_device(): every = lambda v: lax.all_to_all(v, 'fsdp', 0, 0, tiled=True)  25.4 us
    all_to_all x4, waiting for transfers between devices, on_device(): every = lambda v: lax.all_to_all(v, 'fsdp', 0, 0, tiled=True)  21.7 us
    pallas_call x2, Pallas kernels, shampoo(): pl.pallas_call(functools.partial(shampoo_kernel, b, len(bufs)), in_specs=...  19.3 us
    ppermute x10, starting transfers between devices, on_device(): across = lambda v, w: lax.ppermute(v, 'group', w)  16.4 us
    ppermute x10, waiting for transfers between devices, on_device(): across = lambda v, w: lax.ppermute(v, 'group', w)  15.3 us
    pallas_call x3, Pallas kernels, picker(): pl.pallas_call(kernel, in_specs=[SMEM] + [ANY] * (n_in + len(before)), ou...  7.69 us
  transfers between devices with their start and end apart: 42, of which 17 were waited for; matrix products, arithmetic and copies ran while one was open for 0% of the time, Pallas kernels for 21%

profile of v3, /device:TPU:1, one launch (start us, length us, event | category | flops | bytes accessed | tf_op | source)
XLA Modules:
  0.0 225.4 jit_solution(9469793571802939775)
XLA Ops:
  2.8 8.6 %all-to-all-start = ((bf16[32,64,128]{2,1,0:T(8,128)(2,1)}), bf16[32,64,128]{2,1,0:T(8,128)(2,1)S(1)}, u32[]{:S(2)}, u32[]{:S(2)}) async-start(bf16[32,64,128]{2,1,0:T(8,128)(2,1)} %bitcast.3), calls=%async_computation | async-start | bytes 1048576 | tf_op jit(solution)/shard_map/all_to_all | solution.py:586
  12.4 3.0 %tables.1 = (s32[9]{0:T(128)}, s32[2,16]{1,0:T(2,128)}, s32[2,16]{1,0:T(2,128)}, s32[2,16]{1,0:T(2,128)}, s32[2,16]{1,0:T(2,128)}, /*index=5*/s32[2,4]{1,0:T(2,1...) custom-call(s32[4,16]{1,0:T(4,128)} %rows_ref.1, ...), custom_call_target="tpu_custom_call" | custom-call | tf_op jit(solution)/shard_map/tables/pallas_call | solution.py:158
  19.2 4.3 %collective-permute-start.2 = (bf16[2,32,1024]{2,1,0:T(8,128)(2,1)S(1)}, bf16[2,32,1024]{2,1,0:T(8,128)(2,1)S(1)}, u32[]{:S(2)}, u32[]{:S(2)}) collective-permute-start(bf16[2,32,1024]{2,1,0:T(8,128)(2,1)S(1)} %get-tuple-element.66), channel_id=1, source_target_pairs={{1,17},{3,19},{5,21},{7,23},{9,25},{11,27},{13,29},{15,31},{17,1},... | collective-permute-start | bytes 393224 | tf_op jit(solution)/shard_map/ppermute | solution.py:548
  33.8 4.6 %adam.1 = (f32[256,2048]{1,0:T(8,128)}, bf16[16,128]{1,0:T(8,128)(2,1)}) custom-call(bf16[256,2048]{1,0:T(8,128)(2,1)} %g_ref.1, f32[256,2048]{1,0:T(8,128)} %m_ref.1), custom_call_target="tpu_custom_call" | custom-call | tf_op jit(solution)/shard_map/adam/pallas_call | solution.py:58
  39.1 2.8 %pick_for_owners.1 = bf16[32,272,128]{2,1,0:T(8,128)(2,1)} custom-call(s32[32,2]{1,0:T(8,128)S(1)} %copy-done.2, bf16[8,256,128]{2,1,0:T(8,128)(2,1)S(1)} %bitcast.16, bf16[16,128]{1,0:T(8,128)(2,1)S(1)} %copy-done.7), custom_call_target="tpu_custom_call" | custom-call | bytes 3145728 | tf_op jit(solution)/shard_map/pick_for_owners/pallas_call | solution.py:416
  44.4 3.7 %collective-permute-done.4.refs_1_ = bf16[4,2,32,1024]{3,2,1,0:T(8,128)(2,1)S(1)} collective-permute-done((bf16[4,2,32,1024]{3,2,1,0:T(8,128)(2,1)S(1)}, bf16[4,2,32,1024]{3,2,1,0:T(8,128)(2,1)S(1)}, u32[]{:S(2)}, u32[]{:S(2)}) %collective-permute-start.4) | collective-permute-done | bytes 524320 | tf_op jit(solution)/shard_map/ppermute | solution.py:548
  48.1 6.4 %all-to-all-start.1 = ((bf16[32,272,128]{2,1,0:T(8,128)(2,1)}), bf16[32,272,128]{2,1,0:T(8,128)(2,1)}, u32[]{:S(2)}, u32[]{:S(2)}) async-start(bf16[32,272,128]{2,1,0:T(8,128)(2,1)} %pick_for_owners.1), calls=%async_computation.1 | async-start | bytes 4456448 | tf_op jit(solution)/shard_map/all_to_all | solution.py:586
  65.7 18.9 %all-to-all-done.1.norm_ref.refs_0_ = bf16[32,272,128]{2,1,0:T(8,128)(2,1)} async-done(((bf16[32,272,128]{2,1,0:T(8,128)(2,1)}), bf16[32,272,128]{2,1,0:T(8,128)(2,1)}, u32[]{:S(2)}, u32[]{:S(2)}) %all-to-all-start.1) | async-done | bytes 2228256 | tf_op jit(solution)/shard_map/all_to_all | solution.py:586
  88.4 2.9 %collective-permute-start.12 = (bf16[2,2,32,1024]{3,2,1,0:T(8,128)(2,1)S(1)}, bf16[2,2,32,1024]{3,2,1,0:T(8,128)(2,1)S(1)}, u32[]{:S(2)}, u32[]{:S(2)}) collective-permute-start(bf16[2,2,32,1024]{3,2,1,0:T(8,128)(2,1)S(1)} %get-tuple-element.84), channel_id=1, source_target_pairs={{0,5},{1,16},{2,7},{3,18},{4,1},{5,20},{6,3},{7,22},{8,13},{9,24},... | collective-permute-start | bytes 786440 | tf_op jit(solution)/shard_map/ppermute | solution.py:548
  91.3 17.7 %shampoo.2 = bf16[32,256,128]{2,1,0:T(8,128)(2,1)} custom-call(s32[3,2]{1,0:T(4,128)} %get-tuple-element.62.mine_ref, s32[32]{0:T(128)} %get-tuple-element.63.off_ref, bf16[32,272,128]{2,1,0:T(8,128)(2,1)} %all-to-all-done.1.norm_ref.refs_0_, f32[1,1,2,1024,1024]{4,3,2,1,0:T(8,128)} %left_ref.3, f32[1,1,2,1024,1024]{4,3,2,1,0:T(8,128)} %right_ref.3, ...), custom_call_target="tpu_custom_call" | custom-call | flops 10737418240 | bytes 12582912 | tf_op jit(solution)/shard_map/shampoo/pallas_call | solution.py:373
  110.2 3.8 %all-to-all-start.2 = ((bf16[32,256,128]{2,1,0:T(8,128)(2,1)}), bf16[32,256,128]{2,1,0:T(8,128)(2,1)S(1)}, u32[]{:S(2)}, u32[]{:S(2)}) async-start(bf16[32,256,128]{2,1,0:T(8,128)(2,1)} %shampoo.2), calls=%async_computation.2 | async-start | bytes 4194304 | tf_op jit(solution)/shard_map/all_to_all | solution.py:586
  115.7 18.6 %collective-permute-start.14 = (bf16[2,2,32,1024]{3,2,1,0:T(8,128)(2,1)}, bf16[2,2,32,1024]{3,2,1,0:T(8,128)(2,1)S(1)}, u32[]{:S(2)}, u32[]{:S(2)}) collective-permute-start(bf16[2,2,32,1024]{3,2,1,0:T(8,128)(2,1)} %get-tuple-element.94), channel_id=1, source_target_pairs={{0,6},{1,25},{2,0},{3,27},{4,2},{5,29},{6,4},{7,31},{8,14},{9,1},{... | collective-permute-start | bytes 786440 | tf_op jit(solution)/shard_map/ppermute | solution.py:548
  134.9 3.3 %collective-permute-start.18 = (bf16[2,2,32,1024]{3,2,1,0:T(8,128)(2,1)}, bf16[2,2,32,1024]{3,2,1,0:T(8,128)(2,1)}, u32[]{:S(2)}, u32[]{:S(2)}) collective-permute-start(bf16[2,2,32,1024]{3,2,1,0:T(8,128)(2,1)} %get-tuple-element.98), channel_id=1, source_target_pairs={{0,25},{1,6},{2,27},{3,0},{4,29},{5,2},{6,31},{7,4},{8,1},{9,14},{... | collective-permute-start | bytes 786440 | tf_op jit(solution)/shard_map/ppermute | solution.py:548
  138.2 5.9 %collective-permute-done.14.refs_1_ = bf16[2,2,32,1024]{3,2,1,0:T(8,128)(2,1)S(1)} collective-permute-done((bf16[2,2,32,1024]{3,2,1,0:T(8,128)(2,1)}, bf16[2,2,32,1024]{3,2,1,0:T(8,128)(2,1)S(1)}, u32[]{:S(2)}, u32[]{:S(2)}) %collective-permute-start.14) | collective-permute-done | bytes 262176 | tf_op jit(solution)/shard_map/ppermute | solution.py:548
  145.8 3.0 %collective-permute-start.20 = (bf16[2,2,32,1024]{3,2,1,0:T(8,128)(2,1)}, bf16[2,2,32,1024]{3,2,1,0:T(8,128)(2,1)}, u32[]{:S(2)}, u32[]{:S(2)}) collective-permute-start(bf16[2,2,32,1024]{3,2,1,0:T(8,128)(2,1)} %get-tuple-element.100), channel_id=1, source_target_pairs={{0,9},{1,2},{2,11},{3,4},{4,13},{5,6},{6,15},{7,0},{8,17},{9,10},{... | collective-permute-start | bytes 786440 | tf_op jit(solution)/shard_map/ppermute | solution.py:548
  151.0 6.6 %all-to-all-start.3 = ((bf16[32,64,128]{2,1,0:T(8,128)(2,1)}), bf16[32,64,128]{2,1,0:T(8,128)(2,1)S(1)}, u32[]{:S(2)}, u32[]{:S(2)}) async-start(bf16[32,64,128]{2,1,0:T(8,128)(2,1)} %bitcast.8), calls=%async_computation.3 | async-start | bytes 1048576 | tf_op jit(solution)/shard_map/all_to_all | solution.py:586
  157.7 3.7 %to_homes.1 = (bf16[4,2,32,1024]{3,2,1,0:T(8,128)(2,1)S(1)}, bf16[4,2,32,1024]{3,2,1,0:T(8,128)(2,1)}, bf16[4,2,32,1024]{3,2,1,0:T(8,128)(2,1)}, bf16[4,2,32,1024]{3,2,1,0:T(8,128)(2,1)}) custom-call(s32[2,16]{1,0:T(2,128)S(1)} %copy-done.10, bf16[2,2,32,1024]{3,2,1,0:T(8,128)(2,1)S(1)} %copy-done.1, ...), custom_call_target="tpu_custom_call" | custom-call | bytes 4194304 | tf_op jit(solution)/shard_map/to_homes/pallas_call | solution.py:249
  166.5 2.8 %all-to-all-done.3.own = bf16[32,64,128]{2,1,0:T(8,128)(2,1)S(1)} async-done(((bf16[32,64,128]{2,1,0:T(8,128)(2,1)}), bf16[32,64,128]{2,1,0:T(8,128)(2,1)S(1)}, u32[]{:S(2)}, u32[]{:S(2)}) %all-to-all-start.3) | async-done | bytes 524320 | tf_op jit(solution)/shard_map/all_to_all | solution.py:586
  169.3 3.1 %collective-permute-start.35 = (bf16[32,64,128]{2,1,0:T(8,128)(2,1)S(1)}, bf16[32,64,128]{2,1,0:T(8,128)(2,1)S(1)}, u32[]{:S(2)}, u32[]{:S(2)}) collective-permute-start(bf16[32,64,128]{2,1,0:T(8,128)(2,1)S(1)} %all-to-all-done.3.own), channel_id=1, source_target_pairs={{0,96},{32,0},{64,32},{96,64},{1,97},{33,1},{65,33},{97,65},{2,98}... | collective-permute-start | bytes 1572872 | tf_op jit(solution)/shard_map/ppermute | solution.py:585
  173.9 5.6 %collective-permute-done.22.refs_2_ = bf16[4,2,32,1024]{3,2,1,0:T(8,128)(2,1)S(1)} collective-permute-done((bf16[4,2,32,1024]{3,2,1,0:T(8,128)(2,1)}, bf16[4,2,32,1024]{3,2,1,0:T(8,128)(2,1)S(1)}, u32[]{:S(2)}, u32[]{:S(2)}) %collective-permute-start.22) | collective-permute-done | bytes 524320 | tf_op jit(solution)/shard_map/ppermute | solution.py:548
  187.6 3.3 %collective-permute-done.25.refs_3_ = bf16[2,32,1024]{2,1,0:T(8,128)(2,1)S(1)} collective-permute-done((bf16[2,32,1024]{2,1,0:T(8,128)(2,1)S(1)}, bf16[2,32,1024]{2,1,0:T(8,128)(2,1)S(1)}, u32[]{:S(2)}, u32[]{:S(2)}) %collective-permute-start.25) | collective-permute-done | bytes 131104 | tf_op jit(solution)/shard_map/ppermute | solution.py:548
  194.7 3.1 %collective-permute-start.31 = (bf16[128,1024]{1,0:T(8,128)(2,1)S(1)}, bf16[128,1024]{1,0:T(8,128)(2,1)S(1)}, u32[]{:S(2)}, u32[]{:S(2)}) collective-permute-start(bf16[128,1024]{1,0:T(8,128)(2,1)S(1)} %collective-permute-done.27.refs_1_), channel_id=1, source_target_pairs={{0,96},{32,0},{64,32},{96,64},{1,97},{33,1},{65,33},{97,65},{2,98}... | collective-permute-start | bytes 786440 | tf_op jit(solution)/shard_map/ppermute | solution.py:585
  202.1 5.3 %collective-permute-done.28.refs_2_ = bf16[128,1024]{1,0:T(8,128)(2,1)S(1)} collective-permute-done((bf16[128,1024]{1,0:T(8,128)(2,1)S(1)}, bf16[128,1024]{1,0:T(8,128)(2,1)S(1)}, u32[]{:S(2)}, u32[]{:S(2)}) %collective-permute-start.28) | collective-permute-done | bytes 262176 | tf_op jit(solution)/shard_map/ppermute | solution.py:585
  218.6 4.5 %collective-permute-done.32.refs_6_ = bf16[128,1024]{1,0:T(8,128)(2,1)S(1)} collective-permute-done((bf16[128,1024]{1,0:T(8,128)(2,1)S(1)}, bf16[128,1024]{1,0:T(8,128)(2,1)S(1)}, u32[]{:S(2)}, u32[]{:S(2)}) %collective-permute-start.32) | collective-permute-done | bytes 262176 | tf_op jit(solution)/shard_map/ppermute | solution.py:585
  (122 shorter events, 78.4 us)
Async XLA Ops:
  2.8 27.6 %all-to-all-start = ((bf16[32,64,128]{2,1,0:T(8,128)(2,1)}), bf16[32,64,128]{2,1,0:T(8,128)(2,1)S(1)}, u32[]{:S(2)}, u32[]{:S(2)}) async-start(bf16[32,64,128]{2,1,0:T(8,128)(2,1)} %bitcast.3), calls=%async_computation | async-start | bytes 1048576 | tf_op jit(solution)/shard_map/all_to_all | solution.py:586
  30.4 14.0 %collective-permute-start.6 = (bf16[4,2,32,1024]{3,2,1,0:T(8,128)(2,1)S(1)}, bf16[4,2,32,1024]{3,2,1,0:T(8,128)(2,1)S(1)}, u32[]{:S(2)}, u32[]{:S(2)}) collective-permute-start(bf16[4,2,32,1024]{3,2,1,0:T(8,128)(2,1)S(1)} %spread_stack.1.refs_0_), channel_id=1, source_target_pairs={{0,24},{1,7},{2,26},{3,1},{4,28},{5,3},{6,30},{7,5},{8,0},{9,15},{... | collective-permute-start | bytes 1572872 | tf_op jit(solution)/shard_map/ppermute | solution.py:548
  33.2 14.9 %collective-permute-start.4 = (bf16[4,2,32,1024]{3,2,1,0:T(8,128)(2,1)S(1)}, bf16[4,2,32,1024]{3,2,1,0:T(8,128)(2,1)S(1)}, u32[]{:S(2)}, u32[]{:S(2)}) collective-permute-start(bf16[4,2,32,1024]{3,2,1,0:T(8,128)(2,1)S(1)} %spread_stack.1.refs_0_), channel_id=1, source_target_pairs={{0,8},{1,3},{2,10},{3,5},{4,12},{5,7},{6,14},{7,1},{8,16},{9,11},{... | collective-permute-start | bytes 1572872 | tf_op jit(solution)/shard_map/ppermute | solution.py:548
  48.1 36.5 %all-to-all-start.1 = ((bf16[32,272,128]{2,1,0:T(8,128)(2,1)}), bf16[32,272,128]{2,1,0:T(8,128)(2,1)}, u32[]{:S(2)}, u32[]{:S(2)}) async-start(bf16[32,272,128]{2,1,0:T(8,128)(2,1)} %pick_for_owners.1), calls=%async_computation.1 | async-start | bytes 4456448 | tf_op jit(solution)/shard_map/all_to_all | solution.py:586
  57.0 28.1 %collective-permute-start.7 = (bf16[2,2,32,1024]{3,2,1,0:T(8,128)(2,1)}, bf16[2,2,32,1024]{3,2,1,0:T(8,128)(2,1)S(1)}, u32[]{:S(2)}, u32[]{:S(2)}) collective-permute-start(bf16[2,2,32,1024]{3,2,1,0:T(8,128)(2,1)} %get-tuple-element.79), channel_id=1, source_target_pairs={{0,2},{1,9},{2,4},{3,11},{4,6},{5,13},{6,0},{7,15},{8,10},{9,17},{... | collective-permute-start | bytes 786440 | tf_op jit(solution)/shard_map/ppermute | solution.py:548
  58.5 29.9 %collective-permute-start.8 = (bf16[2,2,32,1024]{3,2,1,0:T(8,128)(2,1)}, bf16[2,2,32,1024]{3,2,1,0:T(8,128)(2,1)S(1)}, u32[]{:S(2)}, u32[]{:S(2)}) collective-permute-start(bf16[2,2,32,1024]{3,2,1,0:T(8,128)(2,1)} %get-tuple-element.80), channel_id=1, source_target_pairs={{0,4},{1,17},{2,6},{3,19},{4,0},{5,21},{6,2},{7,23},{8,12},{9,25},... | collective-permute-start | bytes 786440 | tf_op jit(solution)/shard_map/ppermute | solution.py:548
  61.0 48.1 %collective-permute-start.9 = (bf16[2,2,32,1024]{3,2,1,0:T(8,128)(2,1)}, bf16[2,2,32,1024]{3,2,1,0:T(8,128)(2,1)S(1)}, u32[]{:S(2)}, u32[]{:S(2)}) collective-permute-start(bf16[2,2,32,1024]{3,2,1,0:T(8,128)(2,1)} %get-tuple-element.81), channel_id=1, source_target_pairs={{0,6},{1,25},{2,0},{3,27},{4,2},{5,29},{6,4},{7,31},{8,14},{9,1},{... | collective-permute-start | bytes 786440 | tf_op jit(solution)/shard_map/ppermute | solution.py:548
  62.2 47.0 %collective-permute-start.10 = (bf16[2,2,32,1024]{3,2,1,0:T(8,128)(2,1)}, bf16[2,2,32,1024]{3,2,1,0:T(8,128)(2,1)S(1)}, u32[]{:S(2)}, u32[]{:S(2)}) collective-permute-start(bf16[2,2,32,1024]{3,2,1,0:T(8,128)(2,1)} %get-tuple-element.82), channel_id=1, source_target_pairs={{0,1},{1,0},{2,3},{3,2},{4,5},{5,4},{6,7},{7,6},{8,9},{9,8},{10,11... | collective-permute-start | bytes 786440 | tf_op jit(solution)/shard_map/ppermute | solution.py:548
  63.3 45.9 %collective-permute-start.13 = (bf16[2,2,32,1024]{3,2,1,0:T(8,128)(2,1)S(1)}, bf16[2,2,32,1024]{3,2,1,0:T(8,128)(2,1)S(1)}, u32[]{:S(2)}, u32[]{:S(2)}) collective-permute-start(bf16[2,2,32,1024]{3,2,1,0:T(8,128)(2,1)S(1)} %get-tuple-element.76), channel_id=1, source_target_pairs={{0,7},{1,24},{2,1},{3,26},{4,3},{5,28},{6,5},{7,30},{8,15},{9,0},{... | collective-permute-start | bytes 786440 | tf_op jit(solution)/shard_map/ppermute | solution.py:548
  85.1 24.1 %collective-permute-start.11 = (bf16[2,2,32,1024]{3,2,1,0:T(8,128)(2,1)S(1)}, bf16[2,2,32,1024]{3,2,1,0:T(8,128)(2,1)S(1)}, u32[]{:S(2)}, u32[]{:S(2)}) collective-permute-start(bf16[2,2,32,1024]{3,2,1,0:T(8,128)(2,1)S(1)} %get-tuple-element.83), channel_id=1, source_target_pairs={{0,3},{1,8},{2,5},{3,10},{4,7},{5,12},{6,1},{7,14},{8,11},{9,16},{... | collective-permute-start | bytes 786440 | tf_op jit(solution)/shard_map/ppermute | solution.py:548
  88.4 20.8 %collective-permute-start.12 = (bf16[2,2,32,1024]{3,2,1,0:T(8,128)(2,1)S(1)}, bf16[2,2,32,1024]{3,2,1,0:T(8,128)(2,1)S(1)}, u32[]{:S(2)}, u32[]{:S(2)}) collective-permute-start(bf16[2,2,32,1024]{3,2,1,0:T(8,128)(2,1)S(1)} %get-tuple-element.84), channel_id=1, source_target_pairs={{0,5},{1,16},{2,7},{3,18},{4,1},{5,20},{6,3},{7,22},{8,13},{9,24},... | collective-permute-start | bytes 786440 | tf_op jit(solution)/shard_map/ppermute | solution.py:548
  110.2 38.6 %all-to-all-start.2 = ((bf16[32,256,128]{2,1,0:T(8,128)(2,1)}), bf16[32,256,128]{2,1,0:T(8,128)(2,1)S(1)}, u32[]{:S(2)}, u32[]{:S(2)}) async-start(bf16[32,256,128]{2,1,0:T(8,128)(2,1)} %shampoo.2), calls=%async_computation.2 | async-start | bytes 4194304 | tf_op jit(solution)/shard_map/all_to_all | solution.py:586
  115.7 28.4 %collective-permute-start.14 = (bf16[2,2,32,1024]{3,2,1,0:T(8,128)(2,1)}, bf16[2,2,32,1024]{3,2,1,0:T(8,128)(2,1)S(1)}, u32[]{:S(2)}, u32[]{:S(2)}) collective-permute-start(bf16[2,2,32,1024]{3,2,1,0:T(8,128)(2,1)} %get-tuple-element.94), channel_id=1, source_target_pairs={{0,6},{1,25},{2,0},{3,27},{4,2},{5,29},{6,4},{7,31},{8,14},{9,1},{... | collective-permute-start | bytes 786440 | tf_op jit(solution)/shard_map/ppermute | solution.py:548
  134.8 22.9 %collective-permute-start.16 = (bf16[2,2,32,1024]{3,2,1,0:T(8,128)(2,1)}, bf16[2,2,32,1024]{3,2,1,0:T(8,128)(2,1)S(1)}, u32[]{:S(2)}, u32[]{:S(2)}) collective-permute-start(bf16[2,2,32,1024]{3,2,1,0:T(8,128)(2,1)} %get-tuple-element.96), channel_id=1, source_target_pairs={{0,2},{1,9},{2,4},{3,11},{4,6},{5,13},{6,0},{7,15},{8,10},{9,17},{... | collective-permute-start | bytes 786440 | tf_op jit(solution)/shard_map/ppermute | solution.py:548
  134.9 22.8 %collective-permute-start.17 = (bf16[2,2,32,1024]{3,2,1,0:T(8,128)(2,1)}, bf16[2,2,32,1024]{3,2,1,0:T(8,128)(2,1)S(1)}, u32[]{:S(2)}, u32[]{:S(2)}) collective-permute-start(bf16[2,2,32,1024]{3,2,1,0:T(8,128)(2,1)} %get-tuple-element.97), channel_id=1, source_target_pairs={{0,1},{1,0},{2,3},{3,2},{4,5},{5,4},{6,7},{7,6},{8,9},{9,8},{10,11... | collective-permute-start | bytes 786440 | tf_op jit(solution)/shard_map/ppermute | solution.py:548
  134.9 22.8 %collective-permute-start.18 = (bf16[2,2,32,1024]{3,2,1,0:T(8,128)(2,1)}, bf16[2,2,32,1024]{3,2,1,0:T(8,128)(2,1)}, u32[]{:S(2)}, u32[]{:S(2)}) collective-permute-start(bf16[2,2,32,1024]{3,2,1,0:T(8,128)(2,1)} %get-tuple-element.98), channel_id=1, source_target_pairs={{0,25},{1,6},{2,27},{3,0},{4,29},{5,2},{6,31},{7,4},{8,1},{9,14},{... | collective-permute-start | bytes 786440 | tf_op jit(solution)/shard_map/ppermute | solution.py:548
  151.0 18.3 %all-to-all-start.3 = ((bf16[32,64,128]{2,1,0:T(8,128)(2,1)}), bf16[32,64,128]{2,1,0:T(8,128)(2,1)S(1)}, u32[]{:S(2)}, u32[]{:S(2)}) async-start(bf16[32,64,128]{2,1,0:T(8,128)(2,1)} %bitcast.8), calls=%async_computation.3 | async-start | bytes 1048576 | tf_op jit(solution)/shard_map/all_to_all | solution.py:586
  162.9 16.6 %collective-permute-start.22 = (bf16[4,2,32,1024]{3,2,1,0:T(8,128)(2,1)}, bf16[4,2,32,1024]{3,2,1,0:T(8,128)(2,1)S(1)}, u32[]{:S(2)}, u32[]{:S(2)}) collective-permute-start(bf16[4,2,32,1024]{3,2,1,0:T(8,128)(2,1)} %get-tuple-element.103), channel_id=1, source_target_pairs={{0,16},{1,5},{2,18},{3,7},{4,20},{5,1},{6,22},{7,3},{8,24},{9,13},... | collective-permute-start | bytes 1572872 | tf_op jit(solution)/shard_map/ppermute | solution.py:548
  165.3 14.2 %collective-permute-start.23 = (bf16[4,2,32,1024]{3,2,1,0:T(8,128)(2,1)}, bf16[4,2,32,1024]{3,2,1,0:T(8,128)(2,1)S(1)}, u32[]{:S(2)}, u32[]{:S(2)}) collective-permute-start(bf16[4,2,32,1024]{3,2,1,0:T(8,128)(2,1)} %get-tuple-element.104), channel_id=1, source_target_pairs={{0,24},{1,7},{2,26},{3,1},{4,28},{5,3},{6,30},{7,5},{8,0},{9,15},{... | collective-permute-start | bytes 1572872 | tf_op jit(solution)/shard_map/ppermute | solution.py:548
  169.3 28.5 %collective-permute-start.35 = (bf16[32,64,128]{2,1,0:T(8,128)(2,1)S(1)}, bf16[32,64,128]{2,1,0:T(8,128)(2,1)S(1)}, u32[]{:S(2)}, u32[]{:S(2)}) collective-permute-start(bf16[32,64,128]{2,1,0:T(8,128)(2,1)S(1)} %all-to-all-done.3.own), channel_id=1, source_target_pairs={{0,96},{32,0},{64,32},{96,64},{1,97},{33,1},{65,33},{97,65},{2,98}... | collective-permute-start | bytes 1572872 | tf_op jit(solution)/shard_map/ppermute | solution.py:585
  186.1 15.7 %collective-permute-start.34 = (bf16[32,64,128]{2,1,0:T(8,128)(2,1)S(1)}, bf16[32,64,128]{2,1,0:T(8,128)(2,1)S(1)}, u32[]{:S(2)}, u32[]{:S(2)}) collective-permute-start(bf16[32,64,128]{2,1,0:T(8,128)(2,1)S(1)} %all-to-all-done.3.own), channel_id=1, source_target_pairs={{0,32},{32,64},{64,96},{96,0},{1,33},{33,65},{65,97},{97,1},{2,34}... | collective-permute-start | bytes 1572872 | tf_op jit(solution)/shard_map/ppermute | solution.py:585
  193.1 14.2 %collective-permute-start.28 = (bf16[128,1024]{1,0:T(8,128)(2,1)S(1)}, bf16[128,1024]{1,0:T(8,128)(2,1)S(1)}, u32[]{:S(2)}, u32[]{:S(2)}) collective-permute-start(bf16[128,1024]{1,0:T(8,128)(2,1)S(1)} %get-tuple-element.109.refs_0_), channel_id=1, source_target_pairs={{0,32},{32,64},{64,96},{96,0},{1,33},{33,65},{65,97},{97,1},{2,34}... | collective-permute-start | bytes 786440 | tf_op jit(solution)/shard_map/ppermute | solution.py:585
  199.5 16.3 %collective-permute-start.30 = (bf16[128,1024]{1,0:T(8,128)(2,1)S(1)}, bf16[128,1024]{1,0:T(8,128)(2,1)S(1)}, u32[]{:S(2)}, u32[]{:S(2)}) collective-permute-start(bf16[128,1024]{1,0:T(8,128)(2,1)S(1)} %get-tuple-element.109.refs_0_), channel_id=1, source_target_pairs={{0,96},{32,0},{64,32},{96,64},{1,97},{33,1},{65,33},{97,65},{2,98}... | collective-permute-start | bytes 786440 | tf_op jit(solution)/shard_map/ppermute | solution.py:585
  207.6 15.5 %collective-permute-start.32 = (bf16[128,1024]{1,0:T(8,128)(2,1)S(1)}, bf16[128,1024]{1,0:T(8,128)(2,1)S(1)}, u32[]{:S(2)}, u32[]{:S(2)}) collective-permute-start(bf16[128,1024]{1,0:T(8,128)(2,1)S(1)} %collective-permute-done.28.refs_2_), channel_id=1, source_target_pairs={{0,32},{32,64},{64,96},{96,0},{1,33},{33,65},{65,97},{97,1},{2,34}... | collective-permute-start | bytes 786440 | tf_op jit(solution)/shard_map/ppermute | solution.py:585
  (38 other events, 539.1 us)

commit v4 on v3

--- a/solution.py
+++ b/solution.py
@@ -644,8 +644,11 @@
     picked0, got = lax.optimization_barrier((picked0, got))
     got0 = every(picked0)
     picked = picker("to_owners", fwd, [stacked, got[1], got[2], got[3]], 8, 2, (2, part, BS))
-    far_pieces = [(0, 1), (0, 3), (1, 1), (1, 3), (0, 2), (1, 2), (1, 0)]
+    picked = list(picked)
+    far_pieces = [(0, 1), (0, 3), (1, 1), (1, 3), (0, 2), (1, 2)]
     bufs = {(0, 0): picked[0]}
+    bufs[1, 0] = along_second(picked[4], 0, 1)
+    picked[2], picked[6], bufs[1, 0] = lax.optimization_barrier((picked[2], picked[6], bufs[1, 0]))
     for f, k in far_pieces:
         bufs[f, k] = along_second(picked[f * 4 + k], k, f)
 
@@ -661,6 +664,9 @@
     update = column_rows(0, cols, groups, far_tab, [home0, before, after, far_lo, far_hi])
 
     back = {(0, 0): done[0]}
+    done = list(done)
+    back[1, 0] = back_second(done[4], 0, 1)
+    done[2], done[6], back[1, 0] = lax.optimization_barrier((done[2], done[6], back[1, 0]))
     for f, k in far_pieces:
         back[f, k] = back_second(done[f * 4 + k], k, f)
     back = [back[f, k] for f in range(2) for k in range(4)]

time: 226 us -> 220 us (0.973)
  starting transfers between devices: 103 us -> 81.8 us
  Pallas kernels: 50.2 us -> 67.3 us
    ppermute x28, starting transfers between devices: 61.4 us -> 39.6 us  [permute(): return lax.ppermute(value, 'fsdp', pairs)]
    pallas_call x2, Pallas kernels: 19.3 us -> 36.1 us  [shampoo(): pl.pallas_call(functools.partial(shampoo_kernel, b, len(bufs)), in_specs=...]
    ppermute x28, waiting for transfers between devices: 27.8 us -> 23.7 us  [permute(): return lax.ppermute(value, 'fsdp', pairs)]
  transfers between devices with their start and end apart: 42 -> 42, of which waited for: 17 -> 17; matrix products, arithmetic and copies ran while one was open for 0% -> 0% of each run, Pallas kernels for 21% -> 30%
where the time goes in v4:
time: 220 us; the launch traced here: 219 us
  starting transfers between devices  81.8 us (37%)
  Pallas kernels  67.3 us (31%)
  waiting for transfers between devices  62.7 us (28%)
  local copies, waits for them, and re-layouts  5.23 us (2%)
    ppermute x28, starting transfers between devices, permute(): return lax.ppermute(value, 'fsdp', pairs)  39.6 us
    pallas_call x2, Pallas kernels, shampoo(): pl.pallas_call(functools.partial(shampoo_kernel, b, len(bufs)), in_specs=...  36.1 us
    all_to_all x4, starting transfers between devices, on_device(): every = lambda v: lax.all_to_all(v, 'fsdp', 0, 0, tiled=True)  24.7 us
    ppermute x28, waiting for transfers between devices, permute(): return lax.ppermute(value, 'fsdp', pairs)  23.7 us
    all_to_all x4, waiting for transfers between devices, on_device(): every = lambda v: lax.all_to_all(v, 'fsdp', 0, 0, tiled=True)  22.4 us
    ppermute x10, starting transfers between devices, on_device(): across = lambda v, w: lax.ppermute(v, 'group', w)  17.5 us
    ppermute x10, waiting for transfers between devices, on_device(): across = lambda v, w: lax.ppermute(v, 'group', w)  16.6 us
    pallas_call x3, Pallas kernels, picker(): pl.pallas_call(kernel, in_specs=[SMEM] + [ANY] * (n_in + len(before)), ou...  7.99 us
  transfers between devices with their start and end apart: 42, of which 17 were waited for; matrix products, arithmetic and copies ran while one was open for 0% of the time, Pallas kernels for 30%

profile of v4, /device:TPU:1, one launch (start us, length us, event | category | flops | bytes accessed | tf_op | source)
XLA Modules:
  0.0 219.0 jit_solution(13735619486380131865)
XLA Ops:
  2.8 8.6 %all-to-all-start = ((bf16[32,64,128]{2,1,0:T(8,128)(2,1)}), bf16[32,64,128]{2,1,0:T(8,128)(2,1)S(1)}, u32[]{:S(2)}, u32[]{:S(2)}) async-start(bf16[32,64,128]{2,1,0:T(8,128)(2,1)} %bitcast.3), calls=%async_computation | async-start | bytes 1048576 | tf_op jit(solution)/shard_map/all_to_all | solution.py:586
  12.4 3.0 %tables.1 = (s32[9]{0:T(128)}, s32[2,16]{1,0:T(2,128)}, s32[2,16]{1,0:T(2,128)}, s32[2,16]{1,0:T(2,128)}, s32[2,16]{1,0:T(2,128)}, /*index=5*/s32[2,4]{1,0:T(2,1...) custom-call(s32[4,16]{1,0:T(4,128)} %rows_ref.1, ...), custom_call_target="tpu_custom_call" | custom-call | tf_op jit(solution)/shard_map/tables/pallas_call | solution.py:158
  19.2 4.3 %collective-permute-start.2 = (bf16[2,32,1024]{2,1,0:T(8,128)(2,1)S(1)}, bf16[2,32,1024]{2,1,0:T(8,128)(2,1)S(1)}, u32[]{:S(2)}, u32[]{:S(2)}) collective-permute-start(bf16[2,32,1024]{2,1,0:T(8,128)(2,1)S(1)} %get-tuple-element.72), channel_id=1, source_target_pairs={{1,17},{3,19},{5,21},{7,23},{9,25},{11,27},{13,29},{15,31},{17,1},... | collective-permute-start | bytes 393224 | tf_op jit(solution)/shard_map/ppermute | solution.py:548
  33.8 4.6 %adam.1 = (f32[256,2048]{1,0:T(8,128)}, bf16[16,128]{1,0:T(8,128)(2,1)}) custom-call(bf16[256,2048]{1,0:T(8,128)(2,1)} %g_ref.1, f32[256,2048]{1,0:T(8,128)} %m_ref.1), custom_call_target="tpu_custom_call" | custom-call | tf_op jit(solution)/shard_map/adam/pallas_call | solution.py:58
  39.1 2.8 %pick_for_owners.1 = bf16[32,272,128]{2,1,0:T(8,128)(2,1)} custom-call(s32[32,2]{1,0:T(8,128)S(1)} %copy-done.2, bf16[8,256,128]{2,1,0:T(8,128)(2,1)S(1)} %bitcast.16, bf16[16,128]{1,0:T(8,128)(2,1)S(1)} %copy-done.7), custom_call_target="tpu_custom_call" | custom-call | bytes 3145728 | tf_op jit(solution)/shard_map/pick_for_owners/pallas_call | solution.py:416
  44.4 3.7 %collective-permute-done.4.refs_1_ = bf16[4,2,32,1024]{3,2,1,0:T(8,128)(2,1)S(1)} collective-permute-done((bf16[4,2,32,1024]{3,2,1,0:T(8,128)(2,1)S(1)}, bf16[4,2,32,1024]{3,2,1,0:T(8,128)(2,1)S(1)}, u32[]{:S(2)}, u32[]{:S(2)}) %collective-permute-start.4) | collective-permute-done | bytes 524320 | tf_op jit(solution)/shard_map/ppermute | solution.py:548
  48.1 6.4 %all-to-all-start.1 = ((bf16[32,272,128]{2,1,0:T(8,128)(2,1)}), bf16[32,272,128]{2,1,0:T(8,128)(2,1)}, u32[]{:S(2)}, u32[]{:S(2)}) async-start(bf16[32,272,128]{2,1,0:T(8,128)(2,1)} %pick_for_owners.1), calls=%async_computation.1 | async-start | bytes 4456448 | tf_op jit(solution)/shard_map/all_to_all | solution.py:586
  54.5 2.9 %to_owners.1 = (bf16[2,2,32,1024]{3,2,1,0:T(8,128)(2,1)S(1)}, bf16[2,2,32,1024]{3,2,1,0:T(8,128)(2,1)}, bf16[2,2,32,1024]{3,2,1,0:T(8,128)(2,1)S(1)}, bf16[2,2,3...) custom-call(s32[2,16]{1,0:T(2,128)S(1)} %copy-done.11, ...), custom_call_target="tpu_custom_call" | custom-call | bytes 4194304 | tf_op jit(solution)/shard_map/to_owners/pallas_call | solution.py:249
  65.1 19.5 %all-to-all-done.1.norm_ref.refs_0_ = bf16[32,272,128]{2,1,0:T(8,128)(2,1)} async-done(((bf16[32,272,128]{2,1,0:T(8,128)(2,1)}), bf16[32,272,128]{2,1,0:T(8,128)(2,1)}, u32[]{:S(2)}, u32[]{:S(2)}) %all-to-all-start.1) | async-done | bytes 2228256 | tf_op jit(solution)/shard_map/all_to_all | solution.py:586
  85.1 3.1 %collective-permute-start.12 = (bf16[2,2,32,1024]{3,2,1,0:T(8,128)(2,1)S(1)}, bf16[2,2,32,1024]{3,2,1,0:T(8,128)(2,1)S(1)}, u32[]{:S(2)}, u32[]{:S(2)}) collective-permute-start(bf16[2,2,32,1024]{3,2,1,0:T(8,128)(2,1)S(1)} %get-tuple-element.93), channel_id=1, source_target_pairs={{0,5},{1,16},{2,7},{3,18},{4,1},{5,20},{6,3},{7,22},{8,13},{9,24},... | collective-permute-start | bytes 786440 | tf_op jit(solution)/shard_map/ppermute | solution.py:548
  88.2 17.7 %shampoo.2 = bf16[32,256,128]{2,1,0:T(8,128)(2,1)} custom-call(s32[3,2]{1,0:T(4,128)} %get-tuple-element.68.mine_ref, s32[32]{0:T(128)} %get-tuple-element.69.off_ref, bf16[32,272,128]{2,1,0:T(8,128)(2,1)} %all-to-all-done.1.norm_ref.refs_0_, f32[1,1,2,1024,1024]{4,3,2,1,0:T(8,128)} %left_ref.3, f32[1,1,2,1024,1024]{4,3,2,1,0:T(8,128)} %right_ref.3, ...), custom_call_target="tpu_custom_call" | custom-call | flops 10737418240 | bytes 12582912 | tf_op jit(solution)/shard_map/shampoo/pallas_call | solution.py:373
  107.1 3.8 %all-to-all-start.2 = ((bf16[32,256,128]{2,1,0:T(8,128)(2,1)}), bf16[32,256,128]{2,1,0:T(8,128)(2,1)S(1)}, u32[]{:S(2)}, u32[]{:S(2)}) async-start(bf16[32,256,128]{2,1,0:T(8,128)(2,1)} %shampoo.2), calls=%async_computation.2 | async-start | bytes 4194304 | tf_op jit(solution)/shard_map/all_to_all | solution.py:586
  110.9 18.3 %shampoo.3 = (bf16[2,2,32,1024]{3,2,1,0:T(8,128)(2,1)}, bf16[2,2,32,1024]{3,2,1,0:T(8,128)(2,1)}, bf16[2,2,32,1024]{3,2,1,0:T(8,128)(2,1)}, bf16[2,2,32,1024]{3,...) custom-call(s32[3,2]{1,0:T(4,128)} %get-tuple-element.68.mine_ref, ...), custom_call_target="tpu_custom_call" | custom-call | flops 10737418240 | bytes 12582912 | tf_op jit(solution)/shard_map/shampoo/pallas_call | solution.py:373
  135.3 5.5 %collective-permute-done.14.refs_1_ = bf16[2,2,32,1024]{3,2,1,0:T(8,128)(2,1)S(1)} collective-permute-done((bf16[2,2,32,1024]{3,2,1,0:T(8,128)(2,1)}, bf16[2,2,32,1024]{3,2,1,0:T(8,128)(2,1)S(1)}, u32[]{:S(2)}, u32[]{:S(2)}) %collective-permute-start.14) | collective-permute-done | bytes 262176 | tf_op jit(solution)/shard_map/ppermute | solution.py:548
  144.8 5.9 %all-to-all-start.3 = ((bf16[32,64,128]{2,1,0:T(8,128)(2,1)}), bf16[32,64,128]{2,1,0:T(8,128)(2,1)S(1)}, u32[]{:S(2)}, u32[]{:S(2)}) async-start(bf16[32,64,128]{2,1,0:T(8,128)(2,1)} %bitcast.8), calls=%async_computation.3 | async-start | bytes 1048576 | tf_op jit(solution)/shard_map/all_to_all | solution.py:586
  150.7 3.7 %to_homes.1 = (bf16[4,2,32,1024]{3,2,1,0:T(8,128)(2,1)S(1)}, bf16[4,2,32,1024]{3,2,1,0:T(8,128)(2,1)}, bf16[4,2,32,1024]{3,2,1,0:T(8,128)(2,1)}, bf16[4,2,32,1024]{3,2,1,0:T(8,128)(2,1)}) custom-call(s32[2,16]{1,0:T(2,128)S(1)} %copy-done.10, bf16[2,2,32,1024]{3,2,1,0:T(8,128)(2,1)S(1)} %copy-done.1, ...), custom_call_target="tpu_custom_call" | custom-call | bytes 4194304 | tf_op jit(solution)/shard_map/to_homes/pallas_call | solution.py:249
  159.5 2.9 %all-to-all-done.3.own = bf16[32,64,128]{2,1,0:T(8,128)(2,1)S(1)} async-done(((bf16[32,64,128]{2,1,0:T(8,128)(2,1)}), bf16[32,64,128]{2,1,0:T(8,128)(2,1)S(1)}, u32[]{:S(2)}, u32[]{:S(2)}) %all-to-all-start.3) | async-done | bytes 524320 | tf_op jit(solution)/shard_map/all_to_all | solution.py:586
  162.3 3.8 %collective-permute-start.35 = (bf16[32,64,128]{2,1,0:T(8,128)(2,1)S(1)}, bf16[32,64,128]{2,1,0:T(8,128)(2,1)S(1)}, u32[]{:S(2)}, u32[]{:S(2)}) collective-permute-start(bf16[32,64,128]{2,1,0:T(8,128)(2,1)S(1)} %all-to-all-done.3.own), channel_id=1, source_target_pairs={{0,96},{32,0},{64,32},{96,64},{1,97},{33,1},{65,33},{97,65},{2,98}... | collective-permute-start | bytes 1572872 | tf_op jit(solution)/shard_map/ppermute | solution.py:585
  166.9 5.6 %collective-permute-done.22.refs_2_ = bf16[4,2,32,1024]{3,2,1,0:T(8,128)(2,1)S(1)} collective-permute-done((bf16[4,2,32,1024]{3,2,1,0:T(8,128)(2,1)}, bf16[4,2,32,1024]{3,2,1,0:T(8,128)(2,1)S(1)}, u32[]{:S(2)}, u32[]{:S(2)}) %collective-permute-start.22) | collective-permute-done | bytes 524320 | tf_op jit(solution)/shard_map/ppermute | solution.py:548
  192.4 3.0 %collective-permute-done.34.before = bf16[32,64,128]{2,1,0:T(8,128)(2,1)S(1)} collective-permute-done((bf16[32,64,128]{2,1,0:T(8,128)(2,1)S(1)}, bf16[32,64,128]{2,1,0:T(8,128)(2,1)S(1)}, u32[]{:S(2)}, u32[]{:S(2)}) %collective-permute-start.34) | collective-permute-done | bytes 524320 | tf_op jit(solution)/shard_map/ppermute | solution.py:585
  195.7 5.2 %collective-permute-done.28.refs_2_ = bf16[128,1024]{1,0:T(8,128)(2,1)S(1)} collective-permute-done((bf16[128,1024]{1,0:T(8,128)(2,1)S(1)}, bf16[128,1024]{1,0:T(8,128)(2,1)S(1)}, u32[]{:S(2)}, u32[]{:S(2)}) %collective-permute-start.28) | collective-permute-done | bytes 262176 | tf_op jit(solution)/shard_map/ppermute | solution.py:585
  202.6 3.4 %collective-permute-start.33 = (bf16[128,1024]{1,0:T(8,128)(2,1)S(1)}, bf16[128,1024]{1,0:T(8,128)(2,1)S(1)}, u32[]{:S(2)}, u32[]{:S(2)}) collective-permute-start(bf16[128,1024]{1,0:T(8,128)(2,1)S(1)} %collective-permute-done.31.refs_5_), channel_id=1, source_target_pairs={{0,96},{32,0},{64,32},{96,64},{1,97},{33,1},{65,33},{97,65},{2,98}... | collective-permute-start | bytes 786440 | tf_op jit(solution)/shard_map/ppermute | solution.py:585
  206.6 2.8 %column_rows.1.refs_8_ = bf16[256,8192]{1,0:T(8,128)(2,1)} custom-call(s32[2,8]{1,0:T(2,128)S(1)} %copy-done.8, bf16[32,64,128]{2,1,0:T(8,128)(2,1)S(1)} %all-to-all-done.3.own, bf16[32,64,128]{2,1,0:T(8,128)(2,1)S(1)} %collective-permute-done.34.before, bf16[32,64,128]{2,1,0:T(8,128)(2,1)S(1)} %collective-permute-done.35.after, ...), custom_call_target="tpu_custom_call" | custom-call | bytes 4194304 | tf_op jit(solution)/shard_map/column_rows/pallas_call | solution.py:483
  212.2 4.4 %collective-permute-done.32.refs_6_ = bf16[128,1024]{1,0:T(8,128)(2,1)S(1)} collective-permute-done((bf16[128,1024]{1,0:T(8,128)(2,1)S(1)}, bf16[128,1024]{1,0:T(8,128)(2,1)S(1)}, u32[]{:S(2)}, u32[]{:S(2)}) %collective-permute-start.32) | collective-permute-done | bytes 262176 | tf_op jit(solution)/shard_map/ppermute | solution.py:585
  (122 shorter events, 72.7 us)
Async XLA Ops:
  2.8 27.6 %all-to-all-start = ((bf16[32,64,128]{2,1,0:T(8,128)(2,1)}), bf16[32,64,128]{2,1,0:T(8,128)(2,1)S(1)}, u32[]{:S(2)}, u32[]{:S(2)}) async-start(bf16[32,64,128]{2,1,0:T(8,128)(2,1)} %bitcast.3), calls=%async_computation | async-start | bytes 1048576 | tf_op jit(solution)/shard_map/all_to_all | solution.py:586
  30.4 14.0 %collective-permute-start.6 = (bf16[4,2,32,1024]{3,2,1,0:T(8,128)(2,1)S(1)}, bf16[4,2,32,1024]{3,2,1,0:T(8,128)(2,1)S(1)}, u32[]{:S(2)}, u32[]{:S(2)}) collective-permute-start(bf16[4,2,32,1024]{3,2,1,0:T(8,128)(2,1)S(1)} %spread_stack.1.refs_0_), channel_id=1, source_target_pairs={{0,24},{1,7},{2,26},{3,1},{4,28},{5,3},{6,30},{7,5},{8,0},{9,15},{... | collective-permute-start | bytes 1572872 | tf_op jit(solution)/shard_map/ppermute | solution.py:548
  33.2 14.9 %collective-permute-start.4 = (bf16[4,2,32,1024]{3,2,1,0:T(8,128)(2,1)S(1)}, bf16[4,2,32,1024]{3,2,1,0:T(8,128)(2,1)S(1)}, u32[]{:S(2)}, u32[]{:S(2)}) collective-permute-start(bf16[4,2,32,1024]{3,2,1,0:T(8,128)(2,1)S(1)} %spread_stack.1.refs_0_), channel_id=1, source_target_pairs={{0,8},{1,3},{2,10},{3,5},{4,12},{5,7},{6,14},{7,1},{8,16},{9,11},{... | collective-permute-start | bytes 1572872 | tf_op jit(solution)/shard_map/ppermute | solution.py:548
  48.1 36.5 %all-to-all-start.1 = ((bf16[32,272,128]{2,1,0:T(8,128)(2,1)}), bf16[32,272,128]{2,1,0:T(8,128)(2,1)}, u32[]{:S(2)}, u32[]{:S(2)}) async-start(bf16[32,272,128]{2,1,0:T(8,128)(2,1)} %pick_for_owners.1), calls=%async_computation.1 | async-start | bytes 4456448 | tf_op jit(solution)/shard_map/all_to_all | solution.py:586
  57.9 27.2 %collective-permute-start.7 = (bf16[2,2,32,1024]{3,2,1,0:T(8,128)(2,1)}, bf16[2,2,32,1024]{3,2,1,0:T(8,128)(2,1)S(1)}, u32[]{:S(2)}, u32[]{:S(2)}) collective-permute-start(bf16[2,2,32,1024]{3,2,1,0:T(8,128)(2,1)} %get-tuple-element.85), channel_id=1, source_target_pairs={{0,2},{1,9},{2,4},{3,11},{4,6},{5,13},{6,0},{7,15},{8,10},{9,17},{... | collective-permute-start | bytes 786440 | tf_op jit(solution)/shard_map/ppermute | solution.py:548
  59.3 46.7 %collective-permute-start.10 = (bf16[2,2,32,1024]{3,2,1,0:T(8,128)(2,1)}, bf16[2,2,32,1024]{3,2,1,0:T(8,128)(2,1)S(1)}, u32[]{:S(2)}, u32[]{:S(2)}) collective-permute-start(bf16[2,2,32,1024]{3,2,1,0:T(8,128)(2,1)} %get-tuple-element.90), channel_id=1, source_target_pairs={{0,6},{1,25},{2,0},{3,27},{4,2},{5,29},{6,4},{7,31},{8,14},{9,1},{... | collective-permute-start | bytes 786440 | tf_op jit(solution)/shard_map/ppermute | solution.py:548
  60.6 45.4 %collective-permute-start.11 = (bf16[2,2,32,1024]{3,2,1,0:T(8,128)(2,1)}, bf16[2,2,32,1024]{3,2,1,0:T(8,128)(2,1)S(1)}, u32[]{:S(2)}, u32[]{:S(2)}) collective-permute-start(bf16[2,2,32,1024]{3,2,1,0:T(8,128)(2,1)} %get-tuple-element.92), channel_id=1, source_target_pairs={{0,3},{1,8},{2,5},{3,10},{4,7},{5,12},{6,1},{7,14},{8,11},{9,16},{... | collective-permute-start | bytes 786440 | tf_op jit(solution)/shard_map/ppermute | solution.py:548
  62.5 43.5 %collective-permute-start.13 = (bf16[2,2,32,1024]{3,2,1,0:T(8,128)(2,1)S(1)}, bf16[2,2,32,1024]{3,2,1,0:T(8,128)(2,1)S(1)}, u32[]{:S(2)}, u32[]{:S(2)}) collective-permute-start(bf16[2,2,32,1024]{3,2,1,0:T(8,128)(2,1)S(1)} %get-tuple-element.82), channel_id=1, source_target_pairs={{0,7},{1,24},{2,1},{3,26},{4,3},{5,28},{6,5},{7,30},{8,15},{9,0},{... | collective-permute-start | bytes 786440 | tf_op jit(solution)/shard_map/ppermute | solution.py:548
  63.9 42.2 %collective-permute-start.9 = (bf16[2,2,32,1024]{3,2,1,0:T(8,128)(2,1)S(1)}, bf16[2,2,32,1024]{3,2,1,0:T(8,128)(2,1)S(1)}, u32[]{:S(2)}, u32[]{:S(2)}) collective-permute-start(bf16[2,2,32,1024]{3,2,1,0:T(8,128)(2,1)S(1)} %get-tuple-element.89), channel_id=1, source_target_pairs={{0,4},{1,17},{2,6},{3,19},{4,0},{5,21},{6,2},{7,23},{8,12},{9,25},... | collective-permute-start | bytes 786440 | tf_op jit(solution)/shard_map/ppermute | solution.py:548
  85.1 20.9 %collective-permute-start.12 = (bf16[2,2,32,1024]{3,2,1,0:T(8,128)(2,1)S(1)}, bf16[2,2,32,1024]{3,2,1,0:T(8,128)(2,1)S(1)}, u32[]{:S(2)}, u32[]{:S(2)}) collective-permute-start(bf16[2,2,32,1024]{3,2,1,0:T(8,128)(2,1)S(1)} %get-tuple-element.93), channel_id=1, source_target_pairs={{0,5},{1,16},{2,7},{3,18},{4,1},{5,20},{6,3},{7,22},{8,13},{9,24},... | collective-permute-start | bytes 786440 | tf_op jit(solution)/shard_map/ppermute | solution.py:548
  107.1 35.5 %all-to-all-start.2 = ((bf16[32,256,128]{2,1,0:T(8,128)(2,1)}), bf16[32,256,128]{2,1,0:T(8,128)(2,1)S(1)}, u32[]{:S(2)}, u32[]{:S(2)}) async-start(bf16[32,256,128]{2,1,0:T(8,128)(2,1)} %shampoo.2), calls=%async_computation.2 | async-start | bytes 4194304 | tf_op jit(solution)/shard_map/all_to_all | solution.py:586
  129.4 21.3 %collective-permute-start.17 = (bf16[2,2,32,1024]{3,2,1,0:T(8,128)(2,1)}, bf16[2,2,32,1024]{3,2,1,0:T(8,128)(2,1)S(1)}, u32[]{:S(2)}, u32[]{:S(2)}) collective-permute-start(bf16[2,2,32,1024]{3,2,1,0:T(8,128)(2,1)} %get-tuple-element.108), channel_id=1, source_target_pairs={{0,2},{1,9},{2,4},{3,11},{4,6},{5,13},{6,0},{7,15},{8,10},{9,17},{... | collective-permute-start | bytes 786440 | tf_op jit(solution)/shard_map/ppermute | solution.py:548
  130.9 19.8 %collective-permute-start.18 = (bf16[2,2,32,1024]{3,2,1,0:T(8,128)(2,1)}, bf16[2,2,32,1024]{3,2,1,0:T(8,128)(2,1)S(1)}, u32[]{:S(2)}, u32[]{:S(2)}) collective-permute-start(bf16[2,2,32,1024]{3,2,1,0:T(8,128)(2,1)} %get-tuple-element.110), channel_id=1, source_target_pairs={{0,25},{1,6},{2,27},{3,0},{4,29},{5,2},{6,31},{7,4},{8,1},{9,14},{... | collective-permute-start | bytes 786440 | tf_op jit(solution)/shard_map/ppermute | solution.py:548
  132.7 18.0 %collective-permute-start.20 = (bf16[2,2,32,1024]{3,2,1,0:T(8,128)(2,1)}, bf16[2,2,32,1024]{3,2,1,0:T(8,128)(2,1)}, u32[]{:S(2)}, u32[]{:S(2)}) collective-permute-start(bf16[2,2,32,1024]{3,2,1,0:T(8,128)(2,1)} %get-tuple-element.112), channel_id=1, source_target_pairs={{0,9},{1,2},{2,11},{3,4},{4,13},{5,6},{6,15},{7,0},{8,17},{9,10},{... | collective-permute-start | bytes 786440 | tf_op jit(solution)/shard_map/ppermute | solution.py:548
  135.3 15.5 %collective-permute-start.16 = (bf16[2,2,32,1024]{3,2,1,0:T(8,128)(2,1)}, bf16[2,2,32,1024]{3,2,1,0:T(8,128)(2,1)}, u32[]{:S(2)}, u32[]{:S(2)}) collective-permute-start(bf16[2,2,32,1024]{3,2,1,0:T(8,128)(2,1)} %get-tuple-element.107), channel_id=1, source_target_pairs={{0,4},{1,17},{2,6},{3,19},{4,0},{5,21},{6,2},{7,23},{8,12},{9,25},... | collective-permute-start | bytes 786440 | tf_op jit(solution)/shard_map/ppermute | solution.py:548
  144.8 17.6 %all-to-all-start.3 = ((bf16[32,64,128]{2,1,0:T(8,128)(2,1)}), bf16[32,64,128]{2,1,0:T(8,128)(2,1)S(1)}, u32[]{:S(2)}, u32[]{:S(2)}) async-start(bf16[32,64,128]{2,1,0:T(8,128)(2,1)} %bitcast.8), calls=%async_computation.3 | async-start | bytes 1048576 | tf_op jit(solution)/shard_map/all_to_all | solution.py:586
  155.9 16.6 %collective-permute-start.22 = (bf16[4,2,32,1024]{3,2,1,0:T(8,128)(2,1)}, bf16[4,2,32,1024]{3,2,1,0:T(8,128)(2,1)S(1)}, u32[]{:S(2)}, u32[]{:S(2)}) collective-permute-start(bf16[4,2,32,1024]{3,2,1,0:T(8,128)(2,1)} %get-tuple-element.115), channel_id=1, source_target_pairs={{0,16},{1,5},{2,18},{3,7},{4,20},{5,1},{6,22},{7,3},{8,24},{9,13},... | collective-permute-start | bytes 1572872 | tf_op jit(solution)/shard_map/ppermute | solution.py:548
  158.3 14.2 %collective-permute-start.23 = (bf16[4,2,32,1024]{3,2,1,0:T(8,128)(2,1)}, bf16[4,2,32,1024]{3,2,1,0:T(8,128)(2,1)S(1)}, u32[]{:S(2)}, u32[]{:S(2)}) collective-permute-start(bf16[4,2,32,1024]{3,2,1,0:T(8,128)(2,1)} %get-tuple-element.116), channel_id=1, source_target_pairs={{0,24},{1,7},{2,26},{3,1},{4,28},{5,3},{6,30},{7,5},{8,0},{9,15},{... | collective-permute-start | bytes 1572872 | tf_op jit(solution)/shard_map/ppermute | solution.py:548
  162.3 29.0 %collective-permute-start.35 = (bf16[32,64,128]{2,1,0:T(8,128)(2,1)S(1)}, bf16[32,64,128]{2,1,0:T(8,128)(2,1)S(1)}, u32[]{:S(2)}, u32[]{:S(2)}) collective-permute-start(bf16[32,64,128]{2,1,0:T(8,128)(2,1)S(1)} %all-to-all-done.3.own), channel_id=1, source_target_pairs={{0,96},{32,0},{64,32},{96,64},{1,97},{33,1},{65,33},{97,65},{2,98}... | collective-permute-start | bytes 1572872 | tf_op jit(solution)/shard_map/ppermute | solution.py:585
  179.1 16.3 %collective-permute-start.34 = (bf16[32,64,128]{2,1,0:T(8,128)(2,1)S(1)}, bf16[32,64,128]{2,1,0:T(8,128)(2,1)S(1)}, u32[]{:S(2)}, u32[]{:S(2)}) collective-permute-start(bf16[32,64,128]{2,1,0:T(8,128)(2,1)S(1)} %all-to-all-done.3.own), channel_id=1, source_target_pairs={{0,32},{32,64},{64,96},{96,0},{1,33},{33,65},{65,97},{97,1},{2,34}... | collective-permute-start | bytes 1572872 | tf_op jit(solution)/shard_map/ppermute | solution.py:585
  186.1 14.9 %collective-permute-start.28 = (bf16[128,1024]{1,0:T(8,128)(2,1)S(1)}, bf16[128,1024]{1,0:T(8,128)(2,1)S(1)}, u32[]{:S(2)}, u32[]{:S(2)}) collective-permute-start(bf16[128,1024]{1,0:T(8,128)(2,1)S(1)} %get-tuple-element.121.refs_0_), channel_id=1, source_target_pairs={{0,32},{32,64},{64,96},{96,0},{1,33},{33,65},{65,97},{97,1},{2,34}... | collective-permute-start | bytes 786440 | tf_op jit(solution)/shard_map/ppermute | solution.py:585
  191.7 17.8 %collective-permute-start.30 = (bf16[128,1024]{1,0:T(8,128)(2,1)S(1)}, bf16[128,1024]{1,0:T(8,128)(2,1)S(1)}, u32[]{:S(2)}, u32[]{:S(2)}) collective-permute-start(bf16[128,1024]{1,0:T(8,128)(2,1)S(1)} %get-tuple-element.121.refs_0_), channel_id=1, source_target_pairs={{0,96},{32,0},{64,32},{96,64},{1,97},{33,1},{65,33},{97,65},{2,98}... | collective-permute-start | bytes 786440 | tf_op jit(solution)/shard_map/ppermute | solution.py:585
  201.3 15.4 %collective-permute-start.32 = (bf16[128,1024]{1,0:T(8,128)(2,1)S(1)}, bf16[128,1024]{1,0:T(8,128)(2,1)S(1)}, u32[]{:S(2)}, u32[]{:S(2)}) collective-permute-start(bf16[128,1024]{1,0:T(8,128)(2,1)S(1)} %collective-permute-done.28.refs_2_), channel_id=1, source_target_pairs={{0,32},{32,64},{64,96},{96,0},{1,33},{33,65},{65,97},{97,1},{2,34}... | collective-permute-start | bytes 786440 | tf_op jit(solution)/shard_map/ppermute | solution.py:585
  202.6 14.1 %collective-permute-start.33 = (bf16[128,1024]{1,0:T(8,128)(2,1)S(1)}, bf16[128,1024]{1,0:T(8,128)(2,1)S(1)}, u32[]{:S(2)}, u32[]{:S(2)}) collective-permute-start(bf16[128,1024]{1,0:T(8,128)(2,1)S(1)} %collective-permute-done.31.refs_5_), channel_id=1, source_target_pairs={{0,96},{32,0},{64,32},{96,64},{1,97},{33,1},{65,33},{97,65},{2,98}... | collective-permute-start | bytes 786440 | tf_op jit(solution)/shard_map/ppermute | solution.py:585
  (38 other events, 495.1 us)
